TPU v7x, 32 devices: a whole 2x2x4 slice. The times are simulated.
32 devices in a mesh: tile: 16 (over z, x, core), dp: 2 (over y).
Axes of the slice: x: 2, y: 2, z: 4, core: 2. Of those that a mesh axis runs over, the one named last changes fastest.
Arguments:
- feature_map: bfloat16 [2, 256, 64, 256], P('dp', 'tile'), may hold values from -6 to 6
- weight: bfloat16 [9, 256, 256], replicated, may hold values from -0.125 to 0.125
- mask_grad: bfloat16 [2, 16, 2, 14, 14, 256], P('dp', 'tile'), may hold values from -6 to 6
- send_count: int32 [2, 16, 2], P('dp', 'tile'), may hold values from 0 to 2, as said below
- send_row: int32 [2, 16, 2, 2], P('dp', 'tile'), may hold values from 0 to 15
- send_col: int32 [2, 16, 2, 2], P('dp', 'tile'), may hold values from 0 to 50
Outputs:
- map_grad: float32 [2, 256, 64, 256], P('dp', 'tile')
- weight_grad: float32 [9, 256, 256], replicated
Inputs may be any that keep to these rules, and one draw needn't show every extreme that they name: `send_count`: in every tile column each head receives exactly 2 live slots in all; one owner image sends 2 * 2 crops in all, one sends none, every other one 2, which is which drawn for each column; in every column some count equals 2.
All inputs are finite; a program needn't handle non-finite values.
Results may differ from a plain program's by a relative error of at most 0.004.
Values may be sent and summed in bfloat16 or wider, within the bound.
A program may use at most 64 MiB of HBM per device.

v0:
```python
import jax
import jax.numpy as jnp
from jax import lax
from jax.sharding import PartitionSpec as P

GELU_SCALE = 0.7978845608
GELU_CUBIC = 0.044715


def shifted(array, axis, by):
    length = lax.axis_size(axis)
    pairs = [(i, i + by) for i in range(length) if 0 <= i + by < length]
    return lax.ppermute(array, axis, pairs)


def gelu_slope(values):
    inner = GELU_SCALE * (values + GELU_CUBIC * values * values * values)
    tangent = jnp.tanh(inner)
    outer = (
        0.5
        * values
        * (1.0 - tangent * tangent)
        * GELU_SCALE
        * (1.0 + 3.0 * GELU_CUBIC * values * values)
    )
    return 0.5 * (1.0 + tangent) + outer


def conv_backward(crops, weight, upstream):
    box_count = crops.shape[0]
    crop_side = crops.shape[1]
    channels = crops.shape[3]
    padded = jnp.pad(crops, ((0, 0), (1, 1), (1, 1), (0, 0)))
    windows = []
    for tap_index in range(9):
        tap_row = tap_index // 3
        tap_col = tap_index % 3
        windows.append(
            padded[:, tap_row : tap_row + crop_side, tap_col : tap_col + crop_side, :].reshape(
                -1, channels
            )
        )
    pre_act = jnp.zeros((windows[0].shape[0], weight.shape[2]), jnp.float32)
    for tap_index in range(9):
        pre_act = pre_act + jnp.dot(
            windows[tap_index], weight[tap_index], preferred_element_type=jnp.float32
        )
    slope = (upstream.reshape(pre_act.shape).astype(jnp.float32) * gelu_slope(pre_act)).astype(
        jnp.bfloat16
    )
    weight_list = []
    for tap_index in range(9):
        weight_list.append(
            lax.dot_general(
                windows[tap_index],
                slope,
                (((0,), (0,)), ((), ())),
                preferred_element_type=jnp.float32,
            )
        )
    weight_terms = jnp.stack(weight_list)
    grad_pad = jnp.zeros((box_count, crop_side + 2, crop_side + 2, channels), jnp.float32)
    for tap_index in range(9):
        tap_row = tap_index // 3
        tap_col = tap_index % 3
        part_grad = lax.dot_general(
            slope, weight[tap_index], (((1,), (1,)), ((), ())), preferred_element_type=jnp.float32
        )
        grad_pad = grad_pad.at[
            :, tap_row : tap_row + crop_side, tap_col : tap_col + crop_side, :
        ].add(part_grad.reshape(box_count, crop_side, crop_side, channels))
    crop_grad = grad_pad[:, 1 : crop_side + 1, 1 : crop_side + 1, :].astype(jnp.bfloat16)
    return (weight_terms, crop_grad)


def selector(live, slot_total):
    ranks = jnp.cumsum(live) - 1
    targets = lax.broadcasted_iota(jnp.int32, (slot_total, live.shape[0]), 0)
    chosen = (ranks[None, :] == targets) & (live[None, :] > 0)
    return chosen.astype(jnp.bfloat16)


def cut_crops(extended, top_rows, left_cols, crop_side):

    def single(top_row, left_col):
        return lax.dynamic_slice(
            extended, (top_row, left_col, top_row * 0), (crop_side, crop_side, extended.shape[2])
        )

    return jax.vmap(single)(top_rows, left_cols)


def add_crops(canvas, pieces, top_rows, left_cols, live):
    crop_side = pieces.shape[1]
    channels = canvas.shape[2]

    def place(slot_index, running):
        anchor = (top_rows[slot_index], left_cols[slot_index], top_rows[slot_index] * 0)
        current = lax.dynamic_slice(running, anchor, (crop_side, crop_side, channels))
        update = current + pieces[slot_index].astype(running.dtype) * live[slot_index]
        return lax.dynamic_update_slice(running, update, anchor)

    return lax.fori_loop(0, pieces.shape[0], place, canvas)


def on_device(feature_map, weight, mask_grad, send_count, send_row, send_col):
    tile_map = feature_map[0]
    tile_height = tile_map.shape[0]
    map_width = tile_map.shape[1]
    channels = tile_map.shape[2]
    boxes_head = mask_grad.shape[2]
    crop_side = mask_grad.shape[3]
    halo_rows = crop_side - 1
    owners = send_row.shape[2]
    slot_cap = send_row.shape[3]
    slot_total = owners * slot_cap
    below = shifted(tile_map[:halo_rows], "tile", -1)
    extended = jnp.concatenate([tile_map, below], 0)
    top_rows = send_row[0, 0].reshape(-1)
    left_cols = send_col[0, 0].reshape(-1)
    slot_iota = lax.broadcasted_iota(jnp.int32, (owners, slot_cap), 1)
    live = (slot_iota < send_count[0, 0][:, None]).astype(jnp.int32)
    upstream = mask_grad[0, 0]
    crops = cut_crops(extended, top_rows, left_cols, crop_side)
    got_crops, got_live = (
        lax.all_to_all(
            crops.reshape(owners, slot_cap, -1), "dp", split_axis=0, concat_axis=0, tiled=True
        ),
        lax.all_to_all(live, "dp", split_axis=0, concat_axis=0, tiled=True),
    )
    picker = selector(got_live.reshape(-1), boxes_head)
    head_crops = jnp.dot(
        picker, got_crops.reshape(slot_total, -1), preferred_element_type=jnp.float32
    ).astype(jnp.bfloat16)
    weight_terms, crop_grad = conv_backward(
        head_crops.reshape(boxes_head, crop_side, crop_side, channels), weight, upstream
    )
    back_slots = jnp.dot(
        picker.T, crop_grad.reshape(boxes_head, -1), preferred_element_type=jnp.float32
    ).astype(jnp.bfloat16)
    slot_grads = lax.all_to_all(
        back_slots.reshape(owners, slot_cap, -1), "dp", split_axis=0, concat_axis=0, tiled=True
    )
    slot_grads = slot_grads.reshape(slot_total, crop_side, crop_side, channels)
    canvas = jnp.zeros((tile_height + halo_rows, map_width, channels), jnp.float32)
    canvas = add_crops(
        canvas, slot_grads, top_rows, left_cols, live.reshape(-1).astype(jnp.float32)
    )
    arriving = shifted(canvas[tile_height:], "tile", 1)
    map_grad = jnp.concatenate([canvas[:halo_rows] + arriving, canvas[halo_rows:tile_height]], 0)
    box_total = boxes_head * lax.axis_size("tile") * lax.axis_size("dp")
    shard = lax.psum_scatter(weight_terms, "tile", scatter_dimension=1, tiled=True)
    shard = lax.psum(shard, "dp")
    summed = lax.all_gather(shard, "tile", axis=1, tiled=True)
    return (map_grad[None], summed / box_total)


def solution(mesh):
    in_specs = (
        P("dp", "tile", None, None),
        P(),
        P("dp", "tile", None, None, None, None),
        P("dp", "tile", None),
        P("dp", "tile", None, None),
        P("dp", "tile", None, None),
    )
    out_specs = (P("dp", "tile", None, None), P())
    return jax.shard_map(
        on_device, mesh=mesh, in_specs=in_specs, out_specs=out_specs, check_vma=False
    )
```

profile of v0, /device:TPU:8, one launch (start us, length us, event | category | flops | bytes accessed | tf_op | source)
XLA Modules:
  0.0 218.3 jit_solution(14825154797622032213)
XLA Ops:
  7.2 1.3 compare_convert_fusion
  8.5 3.2 %all-to-all-start = ((s32[2,1,2]{2,1,0:T(1,128)}), s32[2,1,2]{2,1,0:T(1,128)S(1)}, u32[]{:S(2)}, u32[]{:S(2)}) async-start(s32[2,1,2]{2,1,0:T(1,128)} %compare_convert_fusion), calls=%async_computation | async-start | bytes 2048 | tf_op jit(solution)/shard_map/all_to_all | solution.py:129
  11.7 1.0 slice_bitcast_fusion
  12.8 2.7 %collective-permute-start = (bf16[13,64,256]{2,1,0:T(8,128)(2,1)S(1)}, bf16[13,64,256]{2,1,0:T(8,128)(2,1)S(1)}, u32[]{:S(2)}, u32[]{:S(2)}) collective-permute-start(bf16[13,64,256]{2,1,0:T(8,128)(2,1)S(1)} %slice_bitcast_fusion), channel_id=1, source_target_pairs={{2,0},{4,2},{6,4},{8,6},{10,8},{12,10},{14,12},{16,14},{18,16},{20... | collective-permute-start | bytes 1277960 | tf_op jit(solution)/shard_map/ppermute | solution.py:13
  15.5 0.8 reshape_squeeze.13
  16.3 0.8 reshape_squeeze.14
  17.1 1.0 copy.14
  18.1 0.8 reshape.621
  19.4 0.7 reduce.29
  20.5 0.6 collective-permute-done
  21.2 7.8 %while.24 = (s32[]{:T(128)}, bf16[29,64,256]{2,1,0:T(8,128)(2,1)S(1)}, s32[4,3]{1,0:T(4,128)S(1)}, bf16[4,14,14,256]{3,2,1,0:T(8,128)(2,1)S(1)}, s32[]{:T(128)}) while((s32[]{:T(128)}, bf16[29,64,256]{2,1,0:T(8,128)(2,1)S(1)}, s32[4,3]{1,0:T(4,128)S(1)}, bf16[4,14,14,256]{3,2,1,0:T(8,128)(2,1)S(1)}, s32[]{:T(128)}) %tuple.96), condition=%wide.while_cond.9, body=%wide.while_body.9.sunk | while | flops 2 | bytes 229493 | solution.py:86
  21.2 0.6 fusion.102
  21.8 1.3 bitcast_dynamic-update-slice_fusion.2
  23.8 1.3 bitcast_dynamic-update-slice_fusion.2
  25.1 0.6 fusion.102
  25.7 1.3 bitcast_dynamic-update-slice_fusion.2
  27.1 0.6 fusion.102
  27.7 1.3 bitcast_dynamic-update-slice_fusion.2
  29.0 0.9 reshape.579
  29.9 3.5 %all-to-all-start.1 = ((bf16[2,2,50176]{2,1,0:T(2,128)(2,1)}), bf16[2,2,50176]{2,1,0:T(2,128)(2,1)S(1)}, u32[]{:S(2)}, u32[]{:S(2)}) async-start(bf16[2,2,50176]{2,1,0:T(2,128)(2,1)} %reshape.579), calls=%async_computation.1 | async-start | bytes 802816 | tf_op jit(solution)/shard_map/all_to_all | solution.py:126
  33.4 7.7 %all-to-all-done.1 = bf16[2,2,50176]{2,1,0:T(2,128)(2,1)S(1)} async-done(((bf16[2,2,50176]{2,1,0:T(2,128)(2,1)}), bf16[2,2,50176]{2,1,0:T(2,128)(2,1)S(1)}, u32[]{:S(2)}, u32[]{:S(2)}) %all-to-all-start.1) | async-done | bytes 401440 | tf_op jit(solution)/shard_map/all_to_all | solution.py:126
  42.0 0.9 pad_slice_fusion
  43.0 1.1 reshape.583
  47.1 1.0 fusion.9
  48.1 1.0 fusion.8
  49.1 1.0 fusion.7
  50.1 1.0 fusion.6
  51.0 1.0 fusion.5
  52.0 1.0 fusion.4
  53.0 1.0 fusion.3
  54.0 1.0 fusion.2
  55.0 1.0 fusion.1
  56.7 61.6 %reduce-scatter.2.cloned.1.call-done = f32[9,16,256]{2,1,0:T(8,128)} async-done(((f32[9,256,256]{2,1,0:T(8,128)}), f32[9,16,256]{2,1,0:T(8,128)}) %reduce-scatter.2.cloned.1.call-update) | async-done | bytes 147472 | tf_op jit(solution)/shard_map/reduce_scatter | solution.py:152
  118.3 0.7 fusion.61
  119.2 0.7 and_reduce_fusion
  120.0 21.5 %all-reduce.4.cloned.1.call-done = f32[9,16,256]{2,1,0:T(8,128)} async-done(((f32[9,16,256]{2,1,0:T(8,128)}), f32[9,16,256]{2,1,0:T(8,128)}) %all-reduce.4.cloned.1.call-update) | async-done | bytes 147472 | tf_op jit(solution)/shard_map/psum | solution.py:153
  141.8 1.5 convolution_add_fusion.7
  143.3 1.7 scatter-add.31
  145.0 2.1 fusion
  147.1 1.8 scatter-add.34
  154.0 0.9 reshape.596
  154.9 3.5 %all-to-all-start.2 = ((bf16[2,2,50176]{2,1,0:T(2,128)(2,1)}), bf16[2,2,50176]{2,1,0:T(2,128)(2,1)S(1)}, u32[]{:S(2)}, u32[]{:S(2)}) async-start(bf16[2,2,50176]{2,1,0:T(2,128)(2,1)} %reshape.596), calls=%async_computation.2 | async-start | bytes 802816 | tf_op jit(solution)/shard_map/all_to_all | solution.py:141
  158.5 6.3 %all-to-all-done.2 = bf16[2,2,50176]{2,1,0:T(2,128)(2,1)S(1)} async-done(((bf16[2,2,50176]{2,1,0:T(2,128)(2,1)}), bf16[2,2,50176]{2,1,0:T(2,128)(2,1)S(1)}, u32[]{:S(2)}, u32[]{:S(2)}) %all-to-all-start.2) | async-done | bytes 401440 | tf_op jit(solution)/shard_map/all_to_all | solution.py:141
  165.3 27.0 %while.23 = (s32[]{:T(128)}, f32[29,64,256]{2,1,0:T(8,128)S(1)}, s32[4]{0:T(128)S(1)}, s32[4]{0:T(128)S(1)}, bf16[4,14,14,256]{3,2,1,0:T(8,128)(2,1)S(1)}, /*ind...) while((s32[]{:T(128)}, f32[29,64,256]{2,1,0:T(8,128)S(1)}, s32[4]{0:T(128)S(1)}, ...), condition=%wide.region_3.4_spmd, body=%wide.region_2.3_spmd.sunk | while | flops 150536 | bytes 903393 | solution.py:103
  165.3 0.6 dynamic_slice.45
  167.9 0.6 dynamic_slice.44
  170.4 0.6 dynamic_slice.46
  171.0 0.7 bitcast_add_fusion.2
  172.1 0.6 dynamic_slice.45
  174.6 0.6 dynamic_slice.44
  177.1 0.6 dynamic_slice.46
  177.7 0.7 bitcast_add_fusion.2
  178.8 0.6 dynamic_slice.45
  181.4 0.6 dynamic_slice.44
  183.9 0.6 dynamic_slice.46
  184.5 0.7 bitcast_add_fusion.2
  185.6 0.6 dynamic_slice.45
  188.1 0.6 dynamic_slice.44
  190.6 0.6 dynamic_slice.46
  191.2 0.7 bitcast_add_fusion.2
  192.4 1.9 collective-permute-start.1
  194.3 13.0 %collective-permute-done.1 = f32[13,64,256]{2,1,0:T(8,128)S(1)} collective-permute-done((f32[13,64,256]{2,1,0:T(8,128)S(1)}, f32[13,64,256]{2,1,0:T(8,128)S(1)}, u32[]{:S(2)}, u32[]{:S(2)}) %collective-permute-start.1) | collective-permute-done | bytes 852000 | tf_op jit(solution)/shard_map/ppermute | solution.py:13
  207.4 1.1 maximum_bitcast_fusion
  208.5 3.3 %broadcast_multiply_fusion = f32[9,256,256]{2,1,0:T(8,128)} fusion(f32[9,256,256]{2,1,0:T(8,128)} %all-gather.2.cloned.1.call-done), kind=kLoop, calls=%fused_computation.22 | loop fusion | flops 589824 | bytes 4718592 | tf_op jit(solution)/shard_map/div | solution.py:155
  (97 shorter events, 14.0 us)
Async XLA Ops:
  7.2 14.0 %copy-start.1 = (bf16[1,16,64,256]{3,2,1,0:T(8,128)(2,1)S(1)}, bf16[1,16,64,256]{3,2,1,0:T(8,128)(2,1)}, u32[]{:S(2)}) copy-start(bf16[1,16,64,256]{3,2,1,0:T(8,128)(2,1)} %param.26) | copy-start | bytes 1572868
  8.5 10.4 %all-to-all-start = ((s32[2,1,2]{2,1,0:T(1,128)}), s32[2,1,2]{2,1,0:T(1,128)S(1)}, u32[]{:S(2)}, u32[]{:S(2)}) async-start(s32[2,1,2]{2,1,0:T(1,128)} %compare_convert_fusion), calls=%async_computation | async-start | bytes 2048 | tf_op jit(solution)/shard_map/all_to_all | solution.py:129
  12.8 8.4 %collective-permute-start = (bf16[13,64,256]{2,1,0:T(8,128)(2,1)S(1)}, bf16[13,64,256]{2,1,0:T(8,128)(2,1)S(1)}, u32[]{:S(2)}, u32[]{:S(2)}) collective-permute-start(bf16[13,64,256]{2,1,0:T(8,128)(2,1)S(1)} %slice_bitcast_fusion), channel_id=1, source_target_pairs={{2,0},{4,2},{6,4},{8,6},{10,8},{12,10},{14,12},{16,14},{18,16},{20... | collective-permute-start | bytes 1277960 | tf_op jit(solution)/shard_map/ppermute | solution.py:13
  29.9 11.3 %all-to-all-start.1 = ((bf16[2,2,50176]{2,1,0:T(2,128)(2,1)}), bf16[2,2,50176]{2,1,0:T(2,128)(2,1)S(1)}, u32[]{:S(2)}, u32[]{:S(2)}) async-start(bf16[2,2,50176]{2,1,0:T(2,128)(2,1)} %reshape.579), calls=%async_computation.1 | async-start | bytes 802816 | tf_op jit(solution)/shard_map/all_to_all | solution.py:126
  33.4 84.9 %reduce-scatter.2.cloned.1.call-start = ((), (), s32[]{:S(2)}) async-start(), calls=%async_computation.4 | async-start | bytes 2506752 | tf_op jit(solution)/shard_map/reduce_scatter | solution.py:152
  42.9 1.6 copy-start
  42.9 2.0 copy-start.2
  45.7 1.0 copy-start.4
  46.1 1.0 copy-start.3
  54.0 65.0 %copy-start.6 = (s32[1,1,2,2]{3,2,1,0:T(2,128)S(1)}, s32[1,1,2,2]{3,2,1,0:T(2,128)}, u32[]{:S(2)}) copy-start(s32[1,1,2,2]{3,2,1,0:T(2,128)} %param.30) | copy-start | bytes 52
  54.0 65.1 %copy-start.7 = (s32[1,1,2,2]{3,2,1,0:T(2,128)S(1)}, s32[1,1,2,2]{3,2,1,0:T(2,128)}, u32[]{:S(2)}) copy-start(s32[1,1,2,2]{3,2,1,0:T(2,128)} %param.31) | copy-start | bytes 52
  54.0 65.1 %copy-start.5 = (s32[4]{0:T(128)S(1)}, s32[4]{0:T(128)}, u32[]{:S(2)}) copy-start(s32[4]{0:T(128)} %constant.328.clone.1) | copy-start | bytes 52
  56.0 85.4 %all-reduce.4.cloned.1.call-start = ((), (), s32[]{:S(2)}) async-start(), calls=%async_computation.5 | async-start | bytes 294912 | tf_op jit(solution)/shard_map/psum | solution.py:153
  118.3 90.2 %all-gather.2.cloned.1.call-start = ((), (), s32[]{:S(2)}) async-start(), calls=%async_computation.6 | async-start | bytes 2506752 | tf_op jit(solution)/shard_map/all_gather | solution.py:154
  152.9 5.5 %copy-start.8 = (s32[1,1,2]{2,1,0:T(1,128)S(1)}, s32[1,1,2]{2,1,0:T(1,128)}, u32[]{:S(2)}) copy-start(s32[1,1,2]{2,1,0:T(1,128)} %param.29) | copy-start | bytes 28
  154.9 9.9 %all-to-all-start.2 = ((bf16[2,2,50176]{2,1,0:T(2,128)(2,1)}), bf16[2,2,50176]{2,1,0:T(2,128)(2,1)S(1)}, u32[]{:S(2)}, u32[]{:S(2)}) async-start(bf16[2,2,50176]{2,1,0:T(2,128)(2,1)} %reshape.596), calls=%async_computation.2 | async-start | bytes 802816 | tf_op jit(solution)/shard_map/all_to_all | solution.py:141
  192.4 14.9 %collective-permute-start.1 = (f32[13,64,256]{2,1,0:T(8,128)S(1)}, f32[13,64,256]{2,1,0:T(8,128)S(1)}, u32[]{:S(2)}, u32[]{:S(2)}) collective-permute-start(f32[13,64,256]{2,1,0:T(8,128)S(1)} %slice.420), channel_id=1, source_target_pairs={{0,2},{2,4},{4,6},{6,8},{8,10},{10,12},{12,14},{14,16},{16,18},{18... | collective-permute-start | bytes 2555912 | tf_op jit(solution)/shard_map/ppermute | solution.py:13
Sparse Core Ops, SparseCore 0:
  56.1 62.0 reduce-scatter.1
  120.6 20.7 all-reduce.3
  143.9 41.7 all-gather.1
where the time goes:
time: 219 us; the launch traced here: 218 us
  waiting for transfers between devices  111 us (51%)
  local copies, waits for them, and re-layouts  35 us (16%)
  matrix products  17.2 us (8%)
  loops' own time  15.8 us (7%)
  starting transfers between devices  14.9 us (7%)
  between operations  14.3 us (7%)
  other arithmetic  10.4 us (5%)
    reduce_scatter x1, waiting for transfers between devices, on_device(): lax.psum_scatter(weight_terms, 'tile', scatter_dimension=1, tiled=True)  61.6 us
    psum x1, waiting for transfers between devices, on_device(): shard = lax.psum(shard, 'dp')  21.5 us
    another operation x1, loops' own time, add_crops(): return lax.fori_loop(0, pieces.shape[0], place, canvas)  15.7 us
    ppermute x2, waiting for transfers between devices, shifted(): return lax.ppermute(array, axis, pairs)  13.6 us
    dot_general x9, matrix products, conv_backward(): lax.dot_general(windows[tap_index], slope, (((0,), (0,)), ((), ())), pref...  8.87 us
    all_to_all x1, waiting for transfers between devices, on_device(): lax.all_to_all(crops.reshape(owners, slot_cap, -1), 'dp', split_axis=0, c...  7.74 us
    gather x12, local copies, waits for them, and re-layouts  7.65 us
    scatter-add x9, local copies, waits for them, and re-layouts, conv_backward(): grad_pad = grad_pad.at[:, tap_row:tap_row + crop_side, tap_col:tap_col +...  6.43 us
  transfers between devices with their start and end apart: 8, of which 6 were waited for; matrix products, arithmetic and copies ran while one was open for 16% of the time, Pallas kernels for 0%

commit v1 on v0

v1 whole, which is shorter than its diff:
```python
import functools

import jax
import jax.numpy as jnp
from jax import lax
from jax.experimental import pallas as pl
from jax.experimental.pallas import tpu as pltpu
from jax.sharding import PartitionSpec as P

GELU_SCALE = 0.7978845608
GELU_CUBIC = 0.044715
LANES = 128
EDGE = 8
VMEM_BYTES = 40 * 1024 * 1024
VM = pl.BlockSpec(memory_space=pltpu.VMEM)
SM = pl.BlockSpec(memory_space=pltpu.SMEM)
LOCAL = pltpu.CompilerParams(vmem_limit_bytes=VMEM_BYTES)


def shifted(array, axis, by):
    length = lax.axis_size(axis)
    pairs = [(i, i + by) for i in range(length) if 0 <= i + by < length]
    return lax.ppermute(array, axis, pairs)


def rotated(array, axis, by):
    length = lax.axis_size(axis)
    return lax.ppermute(array, axis, [(i, (i + by) % length) for i in range(length)])


def gelu_slope(values):
    inner = GELU_SCALE * (values + GELU_CUBIC * values * values * values)
    tangent = jnp.tanh(inner)
    outer = (
        0.5
        * values
        * (1.0 - tangent * tangent)
        * GELU_SCALE
        * (1.0 + 3.0 * GELU_CUBIC * values * values)
    )
    return 0.5 * (1.0 + tangent) + outer


def cut_kernel(n, cap, side, wide, me_ref, count_ref, row_ref, col_ref, map_ref, below_ref, own_ref, send_ref, ext):
    height, width = map_ref.shape[0], map_ref.shape[1]
    ext[:height, EDGE : EDGE + width, :] = map_ref[...].astype(jnp.float32)
    ext[height:, EDGE : EDGE + width, :] = below_ref[...].astype(jnp.float32)
    me = me_ref[0]
    span = 2 * wide
    cell = lax.broadcasted_iota(jnp.int32, (wide, map_ref.shape[2]), 0)
    inside = (cell >= 1) & (cell <= side)
    for k in range(n):
        head = lax.rem(me + k, n)
        for r in range(cap):
            slot = head * cap + r
            top, place = row_ref[slot], col_ref[slot] + EDGE - 1
            base = pl.multiple_of(place // 8 * 8, 8)
            back = lax.rem(span - lax.rem(place, 8), span)
            flag = jnp.where(r < count_ref[head], 1.0, 0.0)
            for y in range(side):
                line = pltpu.roll(ext[top + y, pl.ds(base, span), :], back, 0)[:wide]
                line = jnp.where(inside, line, 0.0)
                if y == 0:
                    line = jnp.where(cell == wide - 1, flag, line)
                line = line.astype(jnp.bfloat16)
                if k == 0:
                    own_ref[r, y] = line
                else:
                    send_ref[k - 1, r, y] = line


def conv_kernel(n, cap, boxes, side, wide, me_ref, own_ref, got_ref, weight_ref, up_ref,
                back_own, back_send, terms_ref, slots, shift, x3, s3, sl, cg, picks):
    channels = weight_ref.shape[2]
    area, full = side * wide, (side + 2) * wide
    me = me_ref[0]
    slots[me] = own_ref[...]
    for k in range(1, n):
        slots[lax.rem(me + n - k, n)] = got_ref[k - 1]
    cell = lax.broadcasted_iota(jnp.int32, (1, wide, channels), 1)
    inside = (cell >= 1) & (cell <= side)
    rank = jnp.zeros((1, channels), jnp.float32)
    for i in range(n):
        for r in range(cap):
            flag = slots[i, r, 0][wide - 1 : wide, :].astype(jnp.float32)
            for b in range(boxes):
                picks[b, i * cap + r] = flag * jnp.where(rank == float(b), 1.0, 0.0)
            rank = rank + flag
    shift[...] = jnp.zeros_like(shift)
    for b in range(boxes):
        box = jnp.zeros((side, wide, channels), jnp.float32)
        for i in range(n):
            for r in range(cap):
                box = box + slots[i, r].astype(jnp.float32) * picks[b, i * cap + r][None]
        box = jnp.where(inside, box, 0.0).reshape(area, channels)
        shift[EDGE + wide : EDGE + wide + area, :] = box
        for t in range(3):
            x3[b, :, t * channels : (t + 1) * channels] = shift[
                EDGE - 1 + t : EDGE - 1 + t + full, :
            ].astype(jnp.bfloat16)
        pre = jnp.zeros((area, channels), jnp.float32)
        for a in range(3):
            pre = pre + jnp.dot(
                x3[b, wide * a : wide * a + area, :],
                weight_ref[3 * a : 3 * a + 3].reshape(3 * channels, channels),
                preferred_element_type=jnp.float32,
            )
        slope = (up_ref[b].reshape(area, channels).astype(jnp.float32) * gelu_slope(pre)).astype(jnp.bfloat16)
        sl[b] = slope
        shift[EDGE + wide : EDGE + wide + area, :] = slope.astype(jnp.float32)
        for t in range(3):
            s3[b, :, t * channels : (t + 1) * channels] = shift[
                EDGE + 1 - t : EDGE + 1 - t + full, :
            ].astype(jnp.bfloat16)
        grad = jnp.zeros((area, channels), jnp.float32)
        for a in range(3):
            for t in range(3):
                grad = grad + lax.dot_general(
                    s3[b, wide * (2 - a) : wide * (2 - a) + area, t * channels : (t + 1) * channels],
                    weight_ref[3 * a + t],
                    (((1,), (1,)), ((), ())),
                    preferred_element_type=jnp.float32,
                )
        grad = jnp.where(inside, grad.reshape(side, wide, channels), 0.0)
        cg[b] = grad.astype(jnp.bfloat16)
    for k in range(n):
        i = lax.rem(me + n - k, n)
        for r in range(cap):
            back = jnp.zeros((side, wide, channels), jnp.float32)
            for b in range(boxes):
                back = back + cg[b].astype(jnp.float32) * picks[b, i * cap + r][None]
            if k == 0:
                back_own[r] = back.astype(jnp.bfloat16)
            else:
                back_send[k - 1, r] = back.astype(jnp.bfloat16)
    for a in range(3):
        total = jnp.zeros((3 * channels, channels), jnp.float32)
        for b in range(boxes):
            total = total + lax.dot_general(
                x3[b, wide * a : wide * a + area, :], sl[b], (((0,), (0,)), ((), ())),
                preferred_element_type=jnp.float32,
            )
        depth = 3 * channels
        for h in range(channels // LANES):
            start = h * 3 * depth + a * depth
            terms_ref[start : start + depth, :] = total[:, h * LANES : (h + 1) * LANES]


def paste_kernel(n, cap, side, wide, me_ref, count_ref, row_ref, col_ref, own_ref, got_ref, main_ref, spill_ref, canvas):
    height, width = main_ref.shape[0], main_ref.shape[1]
    canvas[...] = jnp.zeros_like(canvas)
    me = me_ref[0]
    for k in range(n):
        head = lax.rem(me + k, n)
        for r in range(cap):

            @pl.when(r < count_ref[head])
            def _():
                top, place = row_ref[head * cap + r], col_ref[head * cap + r] + EDGE - 1
                base = pl.multiple_of(place // 8 * 8, 8)
                ahead = lax.rem(place, 8)
                for y in range(side):
                    line = (own_ref[r, y] if k == 0 else got_ref[k - 1, r, y]).astype(jnp.float32)
                    line = jnp.concatenate([line, jnp.zeros_like(line)], 0)
                    window = (top + y, pl.ds(base, 2 * wide), slice(None))
                    canvas[window] = canvas[window] + pltpu.roll(line, ahead, 0)

    main_ref[...] = canvas[:height, EDGE : EDGE + width, :]
    spill_ref[...] = canvas[height:, EDGE : EDGE + width, :].astype(spill_ref.dtype)


def bits_of(name, length):
    return [(name, 1 << i) for i in range(length.bit_length() - 1)]


def plan(tiles, heads, rows):
    tile_bits = bits_of("tile", tiles)
    order = tile_bits[:2] + bits_of("dp", heads) + tile_bits[2:]
    steps, size = [], rows
    for index, (name, bit) in enumerate(order):
        halves = size % 32 == 0
        size = size // 2 if halves else size
        narrow = halves and 0 < index < 3
        steps.append((name, bit, halves, size, narrow))
    return steps


def partner_of(name, bit):
    here = lax.axis_index(name)
    side = lax.rem(here // bit, 2)
    return side, {name: here + bit - 2 * bit * side}


def greet(steps):
    barrier = pltpu.get_barrier_semaphore()
    for name, bit, *_ in steps:
        pl.semaphore_signal(
            barrier, inc=1, device_id=partner_of(name, bit)[1], device_id_type=pl.DeviceIdType.MESH
        )
    pl.semaphore_wait(barrier, len(steps))


def scatter_kernel(steps, terms_ref, out_ref, total, send_sem, recv_sem, *bufs):
    count = len(steps)
    landing, staged = bufs[:count], bufs[count:]
    greet(steps)
    total[...] = terms_ref[...]
    base = 0
    stage_at = 0
    for index, (name, bit, halves, size, narrow) in enumerate(steps):
        side, other = partner_of(name, bit)
        if halves:
            keep = pl.multiple_of(base + side * size, 16)
            give = pl.multiple_of(base + (1 - side) * size, 16)
        else:
            keep, give = base, base
        if narrow:
            staged[stage_at][...] = total[pl.ds(give, size), :].astype(jnp.bfloat16)
            source = staged[stage_at]
            stage_at += 1
        else:
            source = total.at[pl.ds(give, size), :]
        copy = pltpu.make_async_remote_copy(
            src_ref=source, dst_ref=landing[index], send_sem=send_sem.at[index], recv_sem=recv_sem.at[index],
            device_id=other, device_id_type=pl.DeviceIdType.MESH,
        )
        copy.start()
        copy.wait()
        total[pl.ds(keep, size), :] = total[pl.ds(keep, size), :] + landing[index][...].astype(jnp.float32)
        base = keep
    out_ref[...] = total[pl.ds(base, steps[-1][3]), :].astype(out_ref.dtype)


def gather_kernel(steps, part_ref, out_ref, whole, send_sem, recv_sem):
    halving = [s for s in steps if s[2]]
    greet(halving)
    bases = [0]
    for name, bit, _, size, _ in halving:
        bases.append(pl.multiple_of(bases[-1] + partner_of(name, bit)[0] * size, 16))
    whole[pl.ds(bases[-1], halving[-1][3]), :] = part_ref[...]
    for index in reversed(range(len(halving))):
        name, bit, _, size, _ = halving[index]
        mine = whole.at[pl.ds(bases[index + 1], size), :]
        copy = pltpu.make_async_remote_copy(
            src_ref=mine, dst_ref=mine, send_sem=send_sem.at[index], recv_sem=recv_sem.at[index],
            device_id=partner_of(name, bit)[1], device_id_type=pl.DeviceIdType.MESH,
        )
        copy.start()
        copy.wait()
    out_ref[...] = whole[...]


def reduce_scatter(terms, tiles, heads):
    rows = terms.shape[0]
    steps = plan(tiles, heads, rows)
    count = len(steps)
    landing = [pltpu.VMEM((s[3], LANES), jnp.bfloat16 if s[4] else jnp.float32) for s in steps]
    staged = [pltpu.VMEM((s[3], LANES), jnp.bfloat16) for s in steps if s[4]]
    return pl.pallas_call(
        functools.partial(scatter_kernel, steps),
        out_shape=jax.ShapeDtypeStruct((steps[-1][3], LANES), jnp.bfloat16),
        in_specs=[VM],
        out_specs=VM,
        scratch_shapes=[
            pltpu.VMEM(terms.shape, jnp.float32),
            pltpu.SemaphoreType.DMA((count,)),
            pltpu.SemaphoreType.DMA((count,)),
            *landing,
            *staged,
        ],
        compiler_params=pltpu.CompilerParams(
            collective_id=0, has_side_effects=True, vmem_limit_bytes=VMEM_BYTES
        ),
        cost_estimate=pl.CostEstimate(flops=10**6, bytes_accessed=50 * 10**6, transcendentals=0),
        name="term_scatter",
    )(terms)


def gather(part, tiles, heads, rows):
    steps = plan(tiles, heads, rows)
    count = len(steps)
    return pl.pallas_call(
        functools.partial(gather_kernel, steps),
        out_shape=jax.ShapeDtypeStruct((rows, LANES), jnp.bfloat16),
        in_specs=[VM],
        out_specs=VM,
        scratch_shapes=[
            pltpu.VMEM((rows, LANES), jnp.bfloat16),
            pltpu.SemaphoreType.DMA((count,)),
            pltpu.SemaphoreType.DMA((count,)),
        ],
        compiler_params=pltpu.CompilerParams(
            collective_id=1, has_side_effects=True, vmem_limit_bytes=VMEM_BYTES
        ),
        cost_estimate=pl.CostEstimate(flops=10**6, bytes_accessed=50 * 10**6, transcendentals=0),
        name="term_gather",
    )(part)


def on_device(feature_map, weight, mask_grad, send_count, send_row, send_col):
    tile_map = feature_map[0]
    height, width, channels = tile_map.shape
    boxes, side = mask_grad.shape[2], mask_grad.shape[3]
    wide = -(-(side + 2) // 16) * 16
    halo = side - 1
    n, cap = send_row.shape[2], send_row.shape[3]
    tiles, heads = lax.axis_size("tile"), lax.axis_size("dp")
    others = max(n - 1, 1)
    below = shifted(tile_map[:halo], "tile", -1)
    me = lax.axis_index("dp").reshape(1)
    counts = send_count.reshape(-1)
    tops, lefts = send_row.reshape(-1), send_col.reshape(-1)
    room = EDGE + width + 2 * EDGE
    own_shape = jax.ShapeDtypeStruct((cap, side, wide, channels), jnp.bfloat16)
    send_shape = jax.ShapeDtypeStruct((others, cap, side, wide, channels), jnp.bfloat16)
    own, send = pl.pallas_call(
        functools.partial(cut_kernel, n, cap, side, wide),
        out_shape=(own_shape, send_shape),
        in_specs=[SM, SM, SM, SM, VM, VM],
        out_specs=(VM, VM),
        scratch_shapes=[pltpu.VMEM((height + halo, room, channels), jnp.float32)],
        compiler_params=LOCAL,
        name="cut",
    )(me, counts, tops, lefts, tile_map, below)

    def swapped(array, sign):
        parts = [rotated(array[k - 1], "dp", sign * k) for k in range(1, n)]
        return jnp.stack(parts) if len(parts) > 1 else parts[0][None]

    got = swapped(send, 1)
    upstream = jnp.pad(mask_grad[0, 0], ((0, 0), (0, 0), (1, wide - side - 1), (0, 0)))
    full = (side + 2) * wide
    rows = 9 * channels * (channels // LANES)
    back_own, back_send, terms = pl.pallas_call(
        functools.partial(conv_kernel, n, cap, boxes, side, wide),
        out_shape=(own_shape, send_shape, jax.ShapeDtypeStruct((rows, LANES), jnp.float32)),
        in_specs=[SM, VM, VM, VM, VM],
        out_specs=(VM, VM, VM),
        scratch_shapes=[
            pltpu.VMEM((n, cap, side, wide, channels), jnp.bfloat16),
            pltpu.VMEM((full + 2 * EDGE, channels), jnp.float32),
            pltpu.VMEM((boxes, full, 3 * channels), jnp.bfloat16),
            pltpu.VMEM((boxes, full, 3 * channels), jnp.bfloat16),
            pltpu.VMEM((boxes, side * wide, channels), jnp.bfloat16),
            pltpu.VMEM((boxes, side, wide, channels), jnp.bfloat16),
            pltpu.VMEM((boxes, n * cap, 1, channels), jnp.float32),
        ],
        compiler_params=LOCAL,
        name="conv",
    )(me, own, got, weight, upstream)
    back_got = swapped(back_send, -1)
    part = reduce_scatter(terms, tiles, heads)
    main, spill = pl.pallas_call(
        functools.partial(paste_kernel, n, cap, side, wide),
        out_shape=(
            jax.ShapeDtypeStruct((height, width, channels), jnp.float32),
            jax.ShapeDtypeStruct((halo, width, channels), jnp.bfloat16),
        ),
        in_specs=[SM, SM, SM, SM, VM, VM],
        out_specs=(VM, VM),
        scratch_shapes=[pltpu.VMEM((height + halo, room, channels), jnp.float32)],
        compiler_params=LOCAL,
        name="paste",
    )(me, counts, tops, lefts, back_own, back_got)
    arriving = shifted(spill, "tile", 1)
    whole = gather(part, tiles, heads, rows)
    map_grad = main.at[:halo].add(arriving.astype(jnp.float32))
    box_total = boxes * tiles * heads
    halves = whole.reshape(channels // LANES, 9 * channels, LANES)
    summed = jnp.concatenate([halves[h] for h in range(channels // LANES)], -1)
    weight_grad = summed.reshape(9, channels, channels).astype(jnp.float32) / box_total
    return (map_grad[None], weight_grad)


def solution(mesh):
    in_specs = (
        P("dp", "tile", None, None),
        P(),
        P("dp", "tile", None, None, None, None),
        P("dp", "tile", None),
        P("dp", "tile", None, None),
        P("dp", "tile", None, None),
    )
    out_specs = (P("dp", "tile", None, None), P())
    return jax.shard_map(
        on_device, mesh=mesh, in_specs=in_specs, out_specs=out_specs, check_vma=False
    )
```

time: 219 us -> 85.2 us (0.39)
  waiting for transfers between devices: 111 us -> 16.2 us
  Pallas kernels: 0 us -> 51.3 us
  local copies, waits for them, and re-layouts: 35 us -> 6.42 us
  matrix products: 17.2 us -> 0 us
  loops' own time: 15.8 us -> 0 us
  between operations: 14.3 us -> 0.75 us
  other arithmetic: 10.4 us -> 1.77 us
  starting transfers between devices: 14.9 us -> 8.17 us
    reduce_scatter x1 -> x0, waiting for transfers between devices: 61.6 us -> none  [on_device(): lax.psum_scatter(weight_terms, 'tile', scatter_dimension=1, tiled=True)]
    pallas_call x0 -> x5, Pallas kernels: none -> 51.3 us  [the longest x1 26.4 us: reduce_scatter(): pl.pallas_call(functools.partial(scatter_kernel, steps), out_shape=jax.Sh...]
    psum x1 -> x0, waiting for transfers between devices: 21.5 us -> none  [on_device(): shard = lax.psum(shard, 'dp')]
    dot_general x29 -> x0, matrix products: 17.2 us -> none  [the longest x9 8.87 us: conv_backward(): lax.dot_general(windows[tap_index], slope, (((0,), (0,)), ((), ())), pref...]
    another operation x2 -> x0, loops' own time: 15.8 us -> none  [the longest x1 15.7 us: add_crops(): return lax.fori_loop(0, pieces.shape[0], place, canvas)]
    all_to_all x3 -> x0, waiting for transfers between devices: 14 us -> none  [the longest x1 7.74 us: on_device(): lax.all_to_all(crops.reshape(owners, slot_cap, -1), 'dp', split_axis=0, c...]
    all_to_all x3 -> x0, starting transfers between devices: 10.1 us -> none  [the longest x1 3.47 us: on_device(): lax.all_to_all(back_slots.reshape(owners, slot_cap, -1), 'dp', split_axis...]
    gather x12 -> x0, local copies, waits for them, and re-layouts: 7.65 us -> none
  transfers between devices with their start and end apart: 8 -> 4, of which waited for: 6 -> 3; matrix products, arithmetic and copies ran while one was open for 16% -> 5% of each run, Pallas kernels for 0% -> 55%
where the time goes in v1:
time: 85.2 us; the launch traced here: 84.7 us
  Pallas kernels  51.3 us (60%)
  waiting for transfers between devices  16.2 us (19%)
  starting transfers between devices  8.17 us (10%)
  local copies, waits for them, and re-layouts  6.42 us (8%)
  other arithmetic  1.77 us (2%)
    pallas_call x1, Pallas kernels, reduce_scatter(): pl.pallas_call(functools.partial(scatter_kernel, steps), out_shape=jax.Sh...  26.4 us
    pallas_call x1, Pallas kernels, gather(): pl.pallas_call(functools.partial(gather_kernel, steps), out_shape=jax.Sha...  19.8 us
    ppermute x2, waiting for transfers between devices, shifted(): return lax.ppermute(array, axis, pairs)  10.3 us
    ppermute x2, waiting for transfers between devices, rotated(): lax.ppermute(array, axis, [(i, (i + by) % length) for i in range(length)])  5.92 us
    ppermute x2, starting transfers between devices, shifted(): return lax.ppermute(array, axis, pairs)  5 us
    unnamed x12, local copies, waits for them, and re-layouts  3.71 us
    ppermute x2, starting transfers between devices, rotated(): lax.ppermute(array, axis, [(i, (i + by) % length) for i in range(length)])  3.17 us
    pallas_call x1, Pallas kernels, on_device(): pl.pallas_call(functools.partial(conv_kernel, n, cap, boxes, side, wide),...  2.99 us
  transfers between devices with their start and end apart: 4, of which 3 were waited for; matrix products, arithmetic and copies ran while one was open for 5% of the time, Pallas kernels for 55%

profile of v1, /device:TPU:8, one launch (start us, length us, event | category | flops | bytes accessed | tf_op | source)
XLA Modules:
  0.0 84.7 jit_solution(8195081949598648265)
XLA Ops:
  0.6 1.0 %slice_bitcast_fusion = bf16[13,64,256]{2,1,0:T(8,128)(2,1)S(1)} fusion(bf16[1,16,64,256]{3,2,1,0:T(8,128)(2,1)} %param.8), kind=kLoop, calls=%fused_computation.2 | loop fusion | bytes 851968 | tf_op jit(solution)/shard_map/slice | solution.py:309
  1.7 2.7 %collective-permute-start = (bf16[13,64,256]{2,1,0:T(8,128)(2,1)S(1)}, bf16[13,64,256]{2,1,0:T(8,128)(2,1)S(1)}, u32[]{:S(2)}, u32[]{:S(2)}) collective-permute-start(bf16[13,64,256]{2,1,0:T(8,128)(2,1)S(1)} %slice_bitcast_fusion), channel_id=1, source_target_pairs={{2,0},{4,2},{6,4},{8,6},{10,8},{12,10},{14,12},{16,14},{18,16},{20... | collective-permute-start | bytes 1277960 | tf_op jit(solution)/shard_map/ppermute | solution.py:23
  4.4 0.8 reshape.61.row_ref
  5.2 0.8 reshape.62.col_ref
  5.9 4.1 %collective-permute-done.below_ref = bf16[13,64,256]{2,1,0:T(8,128)(2,1)S(1)} collective-permute-done((bf16[13,64,256]{2,1,0:T(8,128)(2,1)S(1)}, bf16[13,64,256]{2,1,0:T(8,128)(2,1)S(1)}, u32[]{:S(2)}, u32[]{:S(2)}) %collective-permute-start) | collective-permute-done | bytes 426016 | tf_op jit(solution)/shard_map/ppermute | solution.py:23
  10.0 0.0 copy-start
  10.0 1.0 %copy-done = bf16[1,16,64,256]{3,2,1,0:T(8,128)(2,1)S(1)} copy-done((bf16[1,16,64,256]{3,2,1,0:T(8,128)(2,1)S(1)}, bf16[1,16,64,256]{3,2,1,0:T(8,128)(2,1)}, u32[]{:S(2)}) %copy-start) | copy-done | bytes 524312
  11.1 0.0 copy-start.2
  11.1 0.7 copy-done.2
  11.7 0.0 copy-start.1
  11.7 0.9 %cut.1 = (bf16[2,14,16,256]{3,2,1,0:T(8,128)(2,1)S(1)}, bf16[1,2,14,16,256]{4,3,2,1,0:T(8,128)(2,1)S(1)}) custom-call(s32[1]{0:T(128)} %bitcast.me_ref, s32[2]{0:T(128)S(1)} %bitcast.21, s32[4]{0:T(128)S(1)} %reshape.61.row_ref, s32[4]{0:T(128)S(1)} %reshape.62.col_ref, bf16[16,64,256]{2,1,0:T(8,128)(2,1)S(1)} %bitcast.18, ...), custom_call_target="tpu_custom_call" | custom-call | tf_op jit(solution)/shard_map/cut/pallas_call | solution.py:316
  12.7 1.6 %collective-permute-start.1 = (bf16[2,14,16,256]{3,2,1,0:T(8,128)(2,1)S(1)}, bf16[2,14,16,256]{3,2,1,0:T(8,128)(2,1)S(1)}, u32[]{:S(2)}, u32[]{:S(2)}) collective-permute-start(bf16[2,14,16,256]{3,2,1,0:T(8,128)(2,1)S(1)} %bitcast.24), channel_id=1, source_target_pairs={{0,1},{1,0},{2,3},{3,2},{4,5},{5,4},{6,7},{7,6},{8,9},{9,8},{10,11... | collective-permute-start | bytes 688136 | tf_op jit(solution)/shard_map/ppermute | solution.py:28
  14.3 1.0 %copy.10 = bf16[1,1,2,14,14,256]{5,4,3,2,1,0:T(8,128)(2,1)S(1)} copy(bf16[1,1,2,14,14,256]{5,2,4,3,1,0:T(2,128)(2,1)} %param.10) | data formatting | bytes 401408 | tf_op args[2]
  15.2 0.1 pad.6.up_ref
  15.3 5.9 %collective-permute-done.1 = bf16[2,14,16,256]{3,2,1,0:T(8,128)(2,1)S(1)} collective-permute-done((bf16[2,14,16,256]{3,2,1,0:T(8,128)(2,1)S(1)}, bf16[2,14,16,256]{3,2,1,0:T(8,128)(2,1)S(1)}, u32[]{:S(2)}, u32[]{:S(2)}) %collective-permute-start.1) | collective-permute-done | bytes 229408 | tf_op jit(solution)/shard_map/ppermute | solution.py:28
  21.2 0.0 copy-done.1
  21.2 0.0 copy-start.3
  21.2 3.0 %conv.1 = (bf16[2,14,16,256]{3,2,1,0:T(8,128)(2,1)S(1)}, bf16[1,2,14,16,256]{4,3,2,1,0:T(8,128)(2,1)S(1)}, f32[4608,128]{1,0:T(8,128)S(1)}) custom-call(s32[1]{0:T(128)} %bitcast.me_ref, bf16[2,14,16,256]{3,2,1,0:T(8,128)(2,1)S(1)} %get-tuple-element.21.own_ref, bf16[1,2,14,16,256]{4,3,2,1,0:T(8,128)(2,1)S(1)} %bitcast.20, ...), custom_call_target="tpu_custom_call" | custom-call | tf_op jit(solution)/shard_map/conv/pallas_call | solution.py:334
  24.2 1.6 %collective-permute-start.2 = (bf16[2,14,16,256]{3,2,1,0:T(8,128)(2,1)S(1)}, bf16[2,14,16,256]{3,2,1,0:T(8,128)(2,1)S(1)}, u32[]{:S(2)}, u32[]{:S(2)}) collective-permute-start(bf16[2,14,16,256]{3,2,1,0:T(8,128)(2,1)S(1)} %bitcast.23), channel_id=1, source_target_pairs={{0,1},{1,0},{2,3},{3,2},{4,5},{5,4},{6,7},{7,6},{8,9},{9,8},{10,11... | collective-permute-start | bytes 688136 | tf_op jit(solution)/shard_map/ppermute | solution.py:28
  25.8 26.4 %term_scatter.1.part_ref = bf16[144,128]{1,0:T(8,128)(2,1)S(1)} custom-call(f32[4608,128]{1,0:T(8,128)S(1)} %get-tuple-element.27.terms_ref), custom_call_target="tpu_custom_call" | custom-call | flops 1000000 | bytes 50000000 | tf_op jit(solution)/shard_map/term_scatter/pallas_call | solution.py:259
  52.2 19.8 %term_gather.1 = bf16[4608,128]{1,0:T(8,128)(2,1)S(1)} custom-call(bf16[144,128]{1,0:T(8,128)(2,1)S(1)} %term_scatter.1.part_ref), custom_call_target="tpu_custom_call" | custom-call | flops 1000000 | bytes 50000000 | tf_op jit(solution)/shard_map/term_gather/pallas_call | solution.py:282
  72.0 0.0 collective-permute-done.2
  72.0 0.0 copy-done.3
  72.0 1.2 %paste.1 = (f32[16,64,256]{2,1,0:T(8,128)S(1)}, bf16[13,64,256]{2,1,0:T(8,128)(2,1)S(1)}) custom-call(s32[1]{0:T(128)} %bitcast.me_ref, s32[2]{0:T(128)S(1)} %bitcast.22, s32[4]{0:T(128)S(1)} %reshape.61.row_ref, s32[4]{0:T(128)S(1)} %reshape.62.col_ref, bf16[2,14,16,256]{3,2,1,0:T(8,128)(2,1)S(1)} %get-tuple-element.23.own_ref, ...), custom_call_target="tpu_custom_call" | custom-call | tf_op jit(solution)/shard_map/paste/pallas_call | solution.py:353
  73.2 2.3 %collective-permute-start.3 = (bf16[13,64,256]{2,1,0:T(8,128)(2,1)S(1)}, bf16[13,64,256]{2,1,0:T(8,128)(2,1)S(1)}, u32[]{:S(2)}, u32[]{:S(2)}) collective-permute-start(bf16[13,64,256]{2,1,0:T(8,128)(2,1)S(1)} %get-tuple-element.26), channel_id=1, source_target_pairs={{0,2},{2,4},{4,6},{6,8},{8,10},{10,12},{12,14},{14,16},{16,18},{18... | collective-permute-start | bytes 1277960 | tf_op jit(solution)/shard_map/ppermute | solution.py:23
  75.5 0.1 fusion
  75.6 1.7 %convert_multiply_fusion = f32[9,256,256]{2,1,0:T(8,128)} fusion(bf16[9,256,128]{2,1,0:T(8,128)(2,1)S(1)} %bitcast.26, bf16[9,256,128]{2,1,0:T(8,128)(2,1)S(1)} %bitcast.25), kind=kLoop, calls=%fused_computation | loop fusion | flops 2949120 | bytes 3538944 | tf_op jit(solution)/shard_map/div | solution.py:371
  77.2 0.1 copy.11
  77.3 6.2 %collective-permute-done.3 = bf16[13,64,256]{2,1,0:T(8,128)(2,1)S(1)} collective-permute-done((bf16[13,64,256]{2,1,0:T(8,128)(2,1)S(1)}, bf16[13,64,256]{2,1,0:T(8,128)(2,1)S(1)}, u32[]{:S(2)}, u32[]{:S(2)}) %collective-permute-start.3) | collective-permute-done | bytes 426016 | tf_op jit(solution)/shard_map/ppermute | solution.py:23
  83.6 0.1 bitcast_dynamic-update-slice_fusion
  83.7 0.0 copy-start.4
  83.7 1.0 %copy-done.4 = f32[1,16,64,256]{3,2,1,0:T(8,128)} copy-done((f32[1,16,64,256]{3,2,1,0:T(8,128)}, f32[1,16,64,256]{3,2,1,0:T(8,128)S(1)}, u32[]{:S(2)}) %copy-start.4) | copy-done | bytes 1048600
Async XLA Ops:
  1.7 8.4 %collective-permute-start = (bf16[13,64,256]{2,1,0:T(8,128)(2,1)S(1)}, bf16[13,64,256]{2,1,0:T(8,128)(2,1)S(1)}, u32[]{:S(2)}, u32[]{:S(2)}) collective-permute-start(bf16[13,64,256]{2,1,0:T(8,128)(2,1)S(1)} %slice_bitcast_fusion), channel_id=1, source_target_pairs={{2,0},{4,2},{6,4},{8,6},{10,8},{12,10},{14,12},{16,14},{18,16},{20... | collective-permute-start | bytes 1277960 | tf_op jit(solution)/shard_map/ppermute | solution.py:23
  10.0 1.0 %copy-start = (bf16[1,16,64,256]{3,2,1,0:T(8,128)(2,1)S(1)}, bf16[1,16,64,256]{3,2,1,0:T(8,128)(2,1)}, u32[]{:S(2)}) copy-start(bf16[1,16,64,256]{3,2,1,0:T(8,128)(2,1)} %param.8) | copy-start | bytes 1572868
  11.1 0.7 copy-start.2
  11.7 9.5 %copy-start.1 = (bf16[9,256,256]{2,1,0:T(8,128)(2,1)S(1)}, bf16[9,256,256]{2,1,0:T(8,128)(2,1)}, u32[]{:S(2)}) copy-start(bf16[9,256,256]{2,1,0:T(8,128)(2,1)} %weight_ref.1) | copy-start | bytes 3538948
  12.7 8.5 %collective-permute-start.1 = (bf16[2,14,16,256]{3,2,1,0:T(8,128)(2,1)S(1)}, bf16[2,14,16,256]{3,2,1,0:T(8,128)(2,1)S(1)}, u32[]{:S(2)}, u32[]{:S(2)}) collective-permute-start(bf16[2,14,16,256]{3,2,1,0:T(8,128)(2,1)S(1)} %bitcast.24), channel_id=1, source_target_pairs={{0,1},{1,0},{2,3},{3,2},{4,5},{5,4},{6,7},{7,6},{8,9},{9,8},{10,11... | collective-permute-start | bytes 688136 | tf_op jit(solution)/shard_map/ppermute | solution.py:28
  21.2 50.8 %copy-start.3 = (s32[1,1,2]{2,1,0:T(1,128)S(1)}, s32[1,1,2]{2,1,0:T(1,128)}, u32[]{:S(2)}) copy-start(s32[1,1,2]{2,1,0:T(1,128)} %param.11) | copy-start | bytes 28
  24.2 47.8 %collective-permute-start.2 = (bf16[2,14,16,256]{3,2,1,0:T(8,128)(2,1)S(1)}, bf16[2,14,16,256]{3,2,1,0:T(8,128)(2,1)S(1)}, u32[]{:S(2)}, u32[]{:S(2)}) collective-permute-start(bf16[2,14,16,256]{3,2,1,0:T(8,128)(2,1)S(1)} %bitcast.23), channel_id=1, source_target_pairs={{0,1},{1,0},{2,3},{3,2},{4,5},{5,4},{6,7},{7,6},{8,9},{9,8},{10,11... | collective-permute-start | bytes 688136 | tf_op jit(solution)/shard_map/ppermute | solution.py:28
  73.2 10.3 %collective-permute-start.3 = (bf16[13,64,256]{2,1,0:T(8,128)(2,1)S(1)}, bf16[13,64,256]{2,1,0:T(8,128)(2,1)S(1)}, u32[]{:S(2)}, u32[]{:S(2)}) collective-permute-start(bf16[13,64,256]{2,1,0:T(8,128)(2,1)S(1)} %get-tuple-element.26), channel_id=1, source_target_pairs={{0,2},{2,4},{4,6},{6,8},{8,10},{10,12},{12,14},{14,16},{16,18},{18... | collective-permute-start | bytes 1277960 | tf_op jit(solution)/shard_map/ppermute | solution.py:23
  83.7 1.0 %copy-start.4 = (f32[1,16,64,256]{3,2,1,0:T(8,128)}, f32[1,16,64,256]{3,2,1,0:T(8,128)S(1)}, u32[]{:S(2)}) copy-start(f32[1,16,64,256]{3,2,1,0:T(8,128)S(1)} %bitcast_dynamic-update-slice_fusion) | copy-start | bytes 3145732

commit v2 on v1

--- a/solution.py
+++ b/solution.py
@@ -173,128 +173,153 @@
     return [(name, 1 << i) for i in range(length.bit_length() - 1)]
 
 
+def part_steps(order, rows):
+    steps, size = [], rows
+    for name, stride, radix in order:
+        if size % (16 * radix) == 0:
+            size = size // radix
+            steps.append((name, stride, radix, True, size))
+        else:
+            digits = radix.bit_length() - 1
+            steps.extend((name, stride << i, 2, False, size) for i in range(digits))
+    return steps
+
+
 def plan(tiles, heads, rows):
-    tile_bits = bits_of("tile", tiles)
-    order = tile_bits[:2] + bits_of("dp", heads) + tile_bits[2:]
-    steps, size = [], rows
-    for index, (name, bit) in enumerate(order):
-        halves = size % 32 == 0
-        size = size // 2 if halves else size
-        narrow = halves and 0 < index < 3
-        steps.append((name, bit, halves, size, narrow))
-    return steps
-
-
-def partner_of(name, bit):
+    tile_bits = [(name, bit, 2) for name, bit in bits_of("tile", tiles)]
+    head_bits = [(name, bit, 2) for name, bit in bits_of("dp", heads)]
+    first, second, far = tile_bits[:1], tile_bits[1:2], tile_bits[2:]
+    if len(far) % 2 == 0:
+        far = [(name, bit, 4) for name, bit, _ in far[::2]]
+    unit = 16 * 32
+    top = -(-(rows // unit) // 2) * unit
+    return [
+        (0, part_steps(first + second + head_bits + far, top)),
+        (top, part_steps(first + head_bits + second + far, rows - top)),
+    ]
+
+
+def peer(name, stride, radix, hop):
     here = lax.axis_index(name)
-    side = lax.rem(here // bit, 2)
-    return side, {name: here + bit - 2 * bit * side}
-
-
-def greet(steps):
+    digit = lax.rem(here // stride, radix)
+    other = lax.rem(digit + hop, radix)
+    return digit, other, {name: here + (other - digit) * stride}
+
+
+def greet(parts):
+    kinds = sorted({step[:3] for _, steps in parts for step in steps})
     barrier = pltpu.get_barrier_semaphore()
-    for name, bit, *_ in steps:
-        pl.semaphore_signal(
-            barrier, inc=1, device_id=partner_of(name, bit)[1], device_id_type=pl.DeviceIdType.MESH
+    count = 0
+    for name, stride, radix in kinds:
+        for hop in range(1, radix):
+            pl.semaphore_signal(
+                barrier, inc=1, device_id=peer(name, stride, radix, hop)[2],
+                device_id_type=pl.DeviceIdType.MESH,
+            )
+            count += 1
+    pl.semaphore_wait(barrier, count)
+
+
+def walk(part_at, begin, steps, landings, stages, terms_ref, total, whole, send_sem, recv_sem):
+    base, wire = begin, 0
+    bases = [begin]
+
+    def copy_to(source, target, device):
+        nonlocal wire
+        copy = pltpu.make_async_remote_copy(
+            src_ref=source, dst_ref=target, send_sem=send_sem.at[part_at, wire], recv_sem=recv_sem.at[part_at, wire],
+            device_id=device, device_id_type=pl.DeviceIdType.MESH,
         )
-    pl.semaphore_wait(barrier, len(steps))
-
-
-def scatter_kernel(steps, terms_ref, out_ref, total, send_sem, recv_sem, *bufs):
-    count = len(steps)
-    landing, staged = bufs[:count], bufs[count:]
-    greet(steps)
-    total[...] = terms_ref[...]
-    base = 0
-    stage_at = 0
-    for index, (name, bit, halves, size, narrow) in enumerate(steps):
-        side, other = partner_of(name, bit)
+        wire += 1
+        copy.start()
+        return copy
+
+    for index, (name, stride, radix, halves, size) in enumerate(steps):
+        held = terms_ref if index == 0 else total
+        copies = []
+        for hop in range(1, radix):
+            digit, other, device = peer(name, stride, radix, hop)
+            give = pl.multiple_of(base + other * size, 16) if halves else base
+            landing = landings[index].at[hop - 1]
+            if halves and index > 0:
+                stage = stages[index].at[hop - 1]
+                stage[...] = held[pl.ds(give, size), :].astype(jnp.bfloat16)
+                copies.append(copy_to(stage, landing, device))
+            else:
+                copies.append(copy_to(held.at[pl.ds(give, size), :], landing, device))
+        yield
+        keep = pl.multiple_of(base + digit * size, 16) if halves else base
+        for copy in copies:
+            copy.wait()
+        value = held[pl.ds(keep, size), :]
+        for hop in range(1, radix):
+            value = value + landings[index][hop - 1].astype(jnp.float32)
+        if index == len(steps) - 1:
+            whole[pl.ds(keep, size), :] = value.astype(jnp.bfloat16)
+        else:
+            total[pl.ds(keep, size), :] = value
         if halves:
-            keep = pl.multiple_of(base + side * size, 16)
-            give = pl.multiple_of(base + (1 - side) * size, 16)
-        else:
-            keep, give = base, base
-        if narrow:
-            staged[stage_at][...] = total[pl.ds(give, size), :].astype(jnp.bfloat16)
-            source = staged[stage_at]
-            stage_at += 1
-        else:
-            source = total.at[pl.ds(give, size), :]
-        copy = pltpu.make_async_remote_copy(
-            src_ref=source, dst_ref=landing[index], send_sem=send_sem.at[index], recv_sem=recv_sem.at[index],
-            device_id=other, device_id_type=pl.DeviceIdType.MESH,
+            bases.append(keep)
+        base = keep
+    halving = [step for step in steps if step[3]]
+    for index in reversed(range(len(halving))):
+        name, stride, radix, _, size = halving[index]
+        mine = whole.at[pl.ds(bases[index + 1], size), :]
+        copies = [
+            copy_to(mine, mine, peer(name, stride, radix, hop)[2]) for hop in range(1, radix)
+        ]
+        yield
+        for copy in copies:
+            copy.wait()
+
+
+def reduce_kernel(parts, layout, terms_ref, out_ref, total, whole, send_sem, recv_sem, *bufs):
+    greet(parts)
+    walks = []
+    for at, (begin, steps) in enumerate(parts):
+        landings, stages = [[bufs[i] if i is not None else None for i in row] for row in layout[at]]
+        walks.append(
+            walk(at, begin, steps, landings, stages, terms_ref, total, whole, send_sem, recv_sem)
         )
-        copy.start()
-        copy.wait()
-        total[pl.ds(keep, size), :] = total[pl.ds(keep, size), :] + landing[index][...].astype(jnp.float32)
-        base = keep
-    out_ref[...] = total[pl.ds(base, steps[-1][3]), :].astype(out_ref.dtype)
-
-
-def gather_kernel(steps, part_ref, out_ref, whole, send_sem, recv_sem):
-    halving = [s for s in steps if s[2]]
-    greet(halving)
-    bases = [0]
-    for name, bit, _, size, _ in halving:
-        bases.append(pl.multiple_of(bases[-1] + partner_of(name, bit)[0] * size, 16))
-    whole[pl.ds(bases[-1], halving[-1][3]), :] = part_ref[...]
-    for index in reversed(range(len(halving))):
-        name, bit, _, size, _ = halving[index]
-        mine = whole.at[pl.ds(bases[index + 1], size), :]
-        copy = pltpu.make_async_remote_copy(
-            src_ref=mine, dst_ref=mine, send_sem=send_sem.at[index], recv_sem=recv_sem.at[index],
-            device_id=partner_of(name, bit)[1], device_id_type=pl.DeviceIdType.MESH,
-        )
-        copy.start()
-        copy.wait()
+    while walks:
+        walks = [w for w in walks if next(w, 0) is None]
     out_ref[...] = whole[...]
 
 
-def reduce_scatter(terms, tiles, heads):
+def reduced(terms, tiles, heads):
     rows = terms.shape[0]
-    steps = plan(tiles, heads, rows)
-    count = len(steps)
-    landing = [pltpu.VMEM((s[3], LANES), jnp.bfloat16 if s[4] else jnp.float32) for s in steps]
-    staged = [pltpu.VMEM((s[3], LANES), jnp.bfloat16) for s in steps if s[4]]
+    parts = plan(tiles, heads, rows)
+    bufs, layout, wires = [], [], 0
+    for _, steps in parts:
+        landings, stages = [], []
+        for index, (_, _, radix, halves, size) in enumerate(steps):
+            narrow = halves and index > 0
+            shape = (radix - 1, size, LANES)
+            landings.append(len(bufs))
+            bufs.append(pltpu.VMEM(shape, jnp.bfloat16 if narrow else jnp.float32))
+            stages.append(len(bufs) if narrow else None)
+            if narrow:
+                bufs.append(pltpu.VMEM(shape, jnp.bfloat16))
+        layout.append((landings, stages))
+        wires = max(wires, sum(s[2] - 1 for s in steps) + sum(s[2] - 1 for s in steps if s[3]))
     return pl.pallas_call(
-        functools.partial(scatter_kernel, steps),
-        out_shape=jax.ShapeDtypeStruct((steps[-1][3], LANES), jnp.bfloat16),
+        functools.partial(reduce_kernel, parts, layout),
+        out_shape=jax.ShapeDtypeStruct((rows, LANES), jnp.bfloat16),
         in_specs=[VM],
         out_specs=VM,
         scratch_shapes=[
             pltpu.VMEM(terms.shape, jnp.float32),
-            pltpu.SemaphoreType.DMA((count,)),
-            pltpu.SemaphoreType.DMA((count,)),
-            *landing,
-            *staged,
+            pltpu.VMEM(terms.shape, jnp.bfloat16),
+            pltpu.SemaphoreType.DMA((len(parts), wires)),
+            pltpu.SemaphoreType.DMA((len(parts), wires)),
+            *bufs,
         ],
         compiler_params=pltpu.CompilerParams(
             collective_id=0, has_side_effects=True, vmem_limit_bytes=VMEM_BYTES
         ),
-        cost_estimate=pl.CostEstimate(flops=10**6, bytes_accessed=50 * 10**6, transcendentals=0),
-        name="term_scatter",
+        cost_estimate=pl.CostEstimate(flops=10**6, bytes_accessed=100 * 10**6, transcendentals=0),
+        name="term_sum",
     )(terms)
-
-
-def gather(part, tiles, heads, rows):
-    steps = plan(tiles, heads, rows)
-    count = len(steps)
-    return pl.pallas_call(
-        functools.partial(gather_kernel, steps),
-        out_shape=jax.ShapeDtypeStruct((rows, LANES), jnp.bfloat16),
-        in_specs=[VM],
-        out_specs=VM,
-        scratch_shapes=[
-            pltpu.VMEM((rows, LANES), jnp.bfloat16),
-            pltpu.SemaphoreType.DMA((count,)),
-            pltpu.SemaphoreType.DMA((count,)),
-        ],
-        compiler_params=pltpu.CompilerParams(
-            collective_id=1, has_side_effects=True, vmem_limit_bytes=VMEM_BYTES
-        ),
-        cost_estimate=pl.CostEstimate(flops=10**6, bytes_accessed=50 * 10**6, transcendentals=0),
-        name="term_gather",
-    )(part)
 
 
 def on_device(feature_map, weight, mask_grad, send_count, send_row, send_col):
@@ -349,7 +374,7 @@
         name="conv",
     )(me, own, got, weight, upstream)
     back_got = swapped(back_send, -1)
-    part = reduce_scatter(terms, tiles, heads)
+    whole = reduced(terms, tiles, heads)
     main, spill = pl.pallas_call(
         functools.partial(paste_kernel, n, cap, side, wide),
         out_shape=(
@@ -363,7 +388,6 @@
         name="paste",
     )(me, counts, tops, lefts, back_own, back_got)
     arriving = shifted(spill, "tile", 1)
-    whole = gather(part, tiles, heads, rows)
     map_grad = main.at[:halo].add(arriving.astype(jnp.float32))
     box_total = boxes * tiles * heads
     halves = whole.reshape(channels // LANES, 9 * channels, LANES)

time: 85.2 us -> 70.7 us (0.83)
  Pallas kernels: 51.3 us -> 37.1 us
    pallas_call x2 -> x1, Pallas kernels: 46.2 us -> 32.3 us  [reduced(): pl.pallas_call(functools.partial(reduce_kernel, parts, layout), out_shape...]
  transfers between devices with their start and end apart: 4 -> 4, of which waited for: 3 -> 3; matrix products, arithmetic and copies ran while one was open for 5% -> 6% of each run, Pallas kernels for 55% -> 46%
where the time goes in v2:
time: 70.7 us; the launch traced here: 70.4 us
  Pallas kernels  37.1 us (52%)
  waiting for transfers between devices  16.2 us (23%)
  starting transfers between devices  8.17 us (12%)
  local copies, waits for them, and re-layouts  6.42 us (9%)
  other arithmetic  1.77 us (3%)
  between operations  0.74 us (1%)
    pallas_call x1, Pallas kernels, reduced(): pl.pallas_call(functools.partial(reduce_kernel, parts, layout), out_shape...  32.3 us
    ppermute x2, waiting for transfers between devices, shifted(): return lax.ppermute(array, axis, pairs)  10.3 us
    ppermute x2, waiting for transfers between devices, rotated(): lax.ppermute(array, axis, [(i, (i + by) % length) for i in range(length)])  5.92 us
    ppermute x2, starting transfers between devices, shifted(): return lax.ppermute(array, axis, pairs)  5 us
    unnamed x12, local copies, waits for them, and re-layouts  3.71 us
    ppermute x2, starting transfers between devices, rotated(): lax.ppermute(array, axis, [(i, (i + by) % length) for i in range(length)])  3.17 us
    pallas_call x1, Pallas kernels, on_device(): pl.pallas_call(functools.partial(conv_kernel, n, cap, boxes, side, wide),...  2.99 us
    div x1, other arithmetic, on_device(): summed.reshape(9, channels, channels).astype(jnp.float32) / box_total  1.66 us
  transfers between devices with their start and end apart: 4, of which 3 were waited for; matrix products, arithmetic and copies ran while one was open for 6% of the time, Pallas kernels for 46%

profile of v2, /device:TPU:8, one launch (start us, length us, event | category | flops | bytes accessed | tf_op | source)
XLA Modules:
  0.0 70.4 jit_solution(6101311899239173066)
XLA Ops:
  0.6 1.0 %slice_bitcast_fusion = bf16[13,64,256]{2,1,0:T(8,128)(2,1)S(1)} fusion(bf16[1,16,64,256]{3,2,1,0:T(8,128)(2,1)} %param.8), kind=kLoop, calls=%fused_computation.2 | loop fusion | bytes 851968 | tf_op jit(solution)/shard_map/slice | solution.py:334
  1.7 2.7 %collective-permute-start = (bf16[13,64,256]{2,1,0:T(8,128)(2,1)S(1)}, bf16[13,64,256]{2,1,0:T(8,128)(2,1)S(1)}, u32[]{:S(2)}, u32[]{:S(2)}) collective-permute-start(bf16[13,64,256]{2,1,0:T(8,128)(2,1)S(1)} %slice_bitcast_fusion), channel_id=1, source_target_pairs={{2,0},{4,2},{6,4},{8,6},{10,8},{12,10},{14,12},{16,14},{18,16},{20... | collective-permute-start | bytes 1277960 | tf_op jit(solution)/shard_map/ppermute | solution.py:23
  4.4 0.8 %reshape.61.row_ref = s32[4]{0:T(128)S(1)} reshape(s32[1,1,2,2]{3,2,1,0:T(2,128)} %param.12) | data formatting | bytes 32 | tf_op jit(solution)/shard_map/reshape | solution.py:337
  5.2 0.8 %reshape.62.col_ref = s32[4]{0:T(128)S(1)} reshape(s32[1,1,2,2]{3,2,1,0:T(2,128)} %param.13) | data formatting | bytes 32 | tf_op jit(solution)/shard_map/reshape | solution.py:337
  5.9 4.1 %collective-permute-done.below_ref = bf16[13,64,256]{2,1,0:T(8,128)(2,1)S(1)} collective-permute-done((bf16[13,64,256]{2,1,0:T(8,128)(2,1)S(1)}, bf16[13,64,256]{2,1,0:T(8,128)(2,1)S(1)}, u32[]{:S(2)}, u32[]{:S(2)}) %collective-permute-start) | collective-permute-done | bytes 426016 | tf_op jit(solution)/shard_map/ppermute | solution.py:23
  10.0 0.0 copy-start
  10.0 1.0 %copy-done = bf16[1,16,64,256]{3,2,1,0:T(8,128)(2,1)S(1)} copy-done((bf16[1,16,64,256]{3,2,1,0:T(8,128)(2,1)S(1)}, bf16[1,16,64,256]{3,2,1,0:T(8,128)(2,1)}, u32[]{:S(2)}) %copy-start) | copy-done | bytes 524312
  11.1 0.0 copy-start.2
  11.1 0.7 copy-done.2
  11.7 0.0 copy-start.1
  11.7 0.9 %cut.1 = (bf16[2,14,16,256]{3,2,1,0:T(8,128)(2,1)S(1)}, bf16[1,2,14,16,256]{4,3,2,1,0:T(8,128)(2,1)S(1)}) custom-call(s32[1]{0:T(128)} %bitcast.me_ref, s32[2]{0:T(128)S(1)} %bitcast.21, s32[4]{0:T(128)S(1)} %reshape.61.row_ref, s32[4]{0:T(128)S(1)} %reshape.62.col_ref, bf16[16,64,256]{2,1,0:T(8,128)(2,1)S(1)} %bitcast.18, ...), custom_call_target="tpu_custom_call" | custom-call | tf_op jit(solution)/shard_map/cut/pallas_call | solution.py:341
  12.7 1.6 %collective-permute-start.1 = (bf16[2,14,16,256]{3,2,1,0:T(8,128)(2,1)S(1)}, bf16[2,14,16,256]{3,2,1,0:T(8,128)(2,1)S(1)}, u32[]{:S(2)}, u32[]{:S(2)}) collective-permute-start(bf16[2,14,16,256]{3,2,1,0:T(8,128)(2,1)S(1)} %bitcast.23), channel_id=1, source_target_pairs={{0,1},{1,0},{2,3},{3,2},{4,5},{5,4},{6,7},{7,6},{8,9},{9,8},{10,11... | collective-permute-start | bytes 688136 | tf_op jit(solution)/shard_map/ppermute | solution.py:28
  14.3 1.0 %copy.10 = bf16[1,1,2,14,14,256]{5,4,3,2,1,0:T(8,128)(2,1)S(1)} copy(bf16[1,1,2,14,14,256]{5,2,4,3,1,0:T(2,128)(2,1)} %param.10) | data formatting | bytes 401408 | tf_op args[2]
  15.2 0.1 pad.6.up_ref
  15.3 5.9 %collective-permute-done.1 = bf16[2,14,16,256]{3,2,1,0:T(8,128)(2,1)S(1)} collective-permute-done((bf16[2,14,16,256]{3,2,1,0:T(8,128)(2,1)S(1)}, bf16[2,14,16,256]{3,2,1,0:T(8,128)(2,1)S(1)}, u32[]{:S(2)}, u32[]{:S(2)}) %collective-permute-start.1) | collective-permute-done | bytes 229408 | tf_op jit(solution)/shard_map/ppermute | solution.py:28
  21.2 0.0 copy-done.1
  21.2 0.0 copy-start.3
  21.2 3.0 %conv.1 = (bf16[2,14,16,256]{3,2,1,0:T(8,128)(2,1)S(1)}, bf16[1,2,14,16,256]{4,3,2,1,0:T(8,128)(2,1)S(1)}, f32[4608,128]{1,0:T(8,128)S(1)}) custom-call(s32[1]{0:T(128)} %bitcast.me_ref, bf16[2,14,16,256]{3,2,1,0:T(8,128)(2,1)S(1)} %get-tuple-element.21.own_ref, bf16[1,2,14,16,256]{4,3,2,1,0:T(8,128)(2,1)S(1)} %bitcast.20, ...), custom_call_target="tpu_custom_call" | custom-call | tf_op jit(solution)/shard_map/conv/pallas_call | solution.py:359
  24.2 1.6 %collective-permute-start.2 = (bf16[2,14,16,256]{3,2,1,0:T(8,128)(2,1)S(1)}, bf16[2,14,16,256]{3,2,1,0:T(8,128)(2,1)S(1)}, u32[]{:S(2)}, u32[]{:S(2)}) collective-permute-start(bf16[2,14,16,256]{3,2,1,0:T(8,128)(2,1)S(1)} %bitcast.24), channel_id=1, source_target_pairs={{0,1},{1,0},{2,3},{3,2},{4,5},{5,4},{6,7},{7,6},{8,9},{9,8},{10,11... | collective-permute-start | bytes 688136 | tf_op jit(solution)/shard_map/ppermute | solution.py:28
  25.8 32.3 %term_sum.1 = bf16[4608,128]{1,0:T(8,128)(2,1)S(1)} custom-call(f32[4608,128]{1,0:T(8,128)S(1)} %get-tuple-element.27.terms_ref), custom_call_target="tpu_custom_call" | custom-call | flops 1000000 | bytes 100000000 | tf_op jit(solution)/shard_map/term_sum/pallas_call | solution.py:305
  58.1 0.0 collective-permute-done.2
  58.1 0.0 copy-done.3
  58.1 0.9 %paste.1 = (f32[16,64,256]{2,1,0:T(8,128)S(1)}, bf16[13,64,256]{2,1,0:T(8,128)(2,1)S(1)}) custom-call(s32[1]{0:T(128)} %bitcast.me_ref, s32[2]{0:T(128)S(1)} %bitcast.22, s32[4]{0:T(128)S(1)} %reshape.61.row_ref, s32[4]{0:T(128)S(1)} %reshape.62.col_ref, bf16[2,14,16,256]{3,2,1,0:T(8,128)(2,1)S(1)} %get-tuple-element.23.own_ref, ...), custom_call_target="tpu_custom_call" | custom-call | tf_op jit(solution)/shard_map/paste/pallas_call | solution.py:378
  59.0 2.3 %collective-permute-start.3 = (bf16[13,64,256]{2,1,0:T(8,128)(2,1)S(1)}, bf16[13,64,256]{2,1,0:T(8,128)(2,1)S(1)}, u32[]{:S(2)}, u32[]{:S(2)}) collective-permute-start(bf16[13,64,256]{2,1,0:T(8,128)(2,1)S(1)} %get-tuple-element.26), channel_id=1, source_target_pairs={{0,2},{2,4},{4,6},{6,8},{8,10},{10,12},{12,14},{14,16},{16,18},{18... | collective-permute-start | bytes 1277960 | tf_op jit(solution)/shard_map/ppermute | solution.py:23
  61.2 0.1 fusion
  61.3 1.7 %convert_multiply_fusion = f32[9,256,256]{2,1,0:T(8,128)} fusion(bf16[9,256,128]{2,1,0:T(8,128)(2,1)S(1)} %bitcast.26, bf16[9,256,128]{2,1,0:T(8,128)(2,1)S(1)} %bitcast.25), kind=kLoop, calls=%fused_computation | loop fusion | flops 2949120 | bytes 3538944 | tf_op jit(solution)/shard_map/div | solution.py:395
  63.0 0.1 copy.11
  63.1 6.2 %collective-permute-done.3 = bf16[13,64,256]{2,1,0:T(8,128)(2,1)S(1)} collective-permute-done((bf16[13,64,256]{2,1,0:T(8,128)(2,1)S(1)}, bf16[13,64,256]{2,1,0:T(8,128)(2,1)S(1)}, u32[]{:S(2)}, u32[]{:S(2)}) %collective-permute-start.3) | collective-permute-done | bytes 426016 | tf_op jit(solution)/shard_map/ppermute | solution.py:23
  69.3 0.1 bitcast_dynamic-update-slice_fusion
  69.4 0.0 copy-start.4
  69.4 1.0 %copy-done.4 = f32[1,16,64,256]{3,2,1,0:T(8,128)} copy-done((f32[1,16,64,256]{3,2,1,0:T(8,128)}, f32[1,16,64,256]{3,2,1,0:T(8,128)S(1)}, u32[]{:S(2)}) %copy-start.4) | copy-done | bytes 1048600
Async XLA Ops:
  1.7 8.4 %collective-permute-start = (bf16[13,64,256]{2,1,0:T(8,128)(2,1)S(1)}, bf16[13,64,256]{2,1,0:T(8,128)(2,1)S(1)}, u32[]{:S(2)}, u32[]{:S(2)}) collective-permute-start(bf16[13,64,256]{2,1,0:T(8,128)(2,1)S(1)} %slice_bitcast_fusion), channel_id=1, source_target_pairs={{2,0},{4,2},{6,4},{8,6},{10,8},{12,10},{14,12},{16,14},{18,16},{20... | collective-permute-start | bytes 1277960 | tf_op jit(solution)/shard_map/ppermute | solution.py:23
  10.0 1.0 %copy-start = (bf16[1,16,64,256]{3,2,1,0:T(8,128)(2,1)S(1)}, bf16[1,16,64,256]{3,2,1,0:T(8,128)(2,1)}, u32[]{:S(2)}) copy-start(bf16[1,16,64,256]{3,2,1,0:T(8,128)(2,1)} %param.8) | copy-start | bytes 1572868
  11.1 0.7 copy-start.2
  11.7 9.5 %copy-start.1 = (bf16[9,256,256]{2,1,0:T(8,128)(2,1)S(1)}, bf16[9,256,256]{2,1,0:T(8,128)(2,1)}, u32[]{:S(2)}) copy-start(bf16[9,256,256]{2,1,0:T(8,128)(2,1)} %weight_ref.1) | copy-start | bytes 3538948
  12.7 8.5 %collective-permute-start.1 = (bf16[2,14,16,256]{3,2,1,0:T(8,128)(2,1)S(1)}, bf16[2,14,16,256]{3,2,1,0:T(8,128)(2,1)S(1)}, u32[]{:S(2)}, u32[]{:S(2)}) collective-permute-start(bf16[2,14,16,256]{3,2,1,0:T(8,128)(2,1)S(1)} %bitcast.23), channel_id=1, source_target_pairs={{0,1},{1,0},{2,3},{3,2},{4,5},{5,4},{6,7},{7,6},{8,9},{9,8},{10,11... | collective-permute-start | bytes 688136 | tf_op jit(solution)/shard_map/ppermute | solution.py:28
  21.2 36.9 %copy-start.3 = (s32[1,1,2]{2,1,0:T(1,128)S(1)}, s32[1,1,2]{2,1,0:T(1,128)}, u32[]{:S(2)}) copy-start(s32[1,1,2]{2,1,0:T(1,128)} %param.11) | copy-start | bytes 28
  24.2 33.9 %collective-permute-start.2 = (bf16[2,14,16,256]{3,2,1,0:T(8,128)(2,1)S(1)}, bf16[2,14,16,256]{3,2,1,0:T(8,128)(2,1)S(1)}, u32[]{:S(2)}, u32[]{:S(2)}) collective-permute-start(bf16[2,14,16,256]{3,2,1,0:T(8,128)(2,1)S(1)} %bitcast.24), channel_id=1, source_target_pairs={{0,1},{1,0},{2,3},{3,2},{4,5},{5,4},{6,7},{7,6},{8,9},{9,8},{10,11... | collective-permute-start | bytes 688136 | tf_op jit(solution)/shard_map/ppermute | solution.py:28
  59.0 10.3 %collective-permute-start.3 = (bf16[13,64,256]{2,1,0:T(8,128)(2,1)S(1)}, bf16[13,64,256]{2,1,0:T(8,128)(2,1)S(1)}, u32[]{:S(2)}, u32[]{:S(2)}) collective-permute-start(bf16[13,64,256]{2,1,0:T(8,128)(2,1)S(1)} %get-tuple-element.26), channel_id=1, source_target_pairs={{0,2},{2,4},{4,6},{6,8},{8,10},{10,12},{12,14},{14,16},{16,18},{18... | collective-permute-start | bytes 1277960 | tf_op jit(solution)/shard_map/ppermute | solution.py:23
  69.4 1.0 %copy-start.4 = (f32[1,16,64,256]{3,2,1,0:T(8,128)}, f32[1,16,64,256]{3,2,1,0:T(8,128)S(1)}, u32[]{:S(2)}) copy-start(f32[1,16,64,256]{3,2,1,0:T(8,128)S(1)} %bitcast_dynamic-update-slice_fusion) | copy-start | bytes 3145732

commit v3 on v2

--- a/solution.py
+++ b/solution.py
@@ -41,7 +41,7 @@
     return 0.5 * (1.0 + tangent) + outer
 
 
-def cut_kernel(n, cap, side, wide, me_ref, count_ref, row_ref, col_ref, map_ref, below_ref, own_ref, send_ref, ext):
+def cut_kernel(n, cap, side, wide, me_ref, slots_ref, map_ref, below_ref, own_ref, send_ref, ext):
     height, width = map_ref.shape[0], map_ref.shape[1]
     ext[:height, EDGE : EDGE + width, :] = map_ref[...].astype(jnp.float32)
     ext[height:, EDGE : EDGE + width, :] = below_ref[...].astype(jnp.float32)
@@ -52,11 +52,10 @@
     for k in range(n):
         head = lax.rem(me + k, n)
         for r in range(cap):
-            slot = head * cap + r
-            top, place = row_ref[slot], col_ref[slot] + EDGE - 1
+            top, place = slots_ref[n + head * cap + r], slots_ref[n + (n + head) * cap + r] + EDGE - 1
             base = pl.multiple_of(place // 8 * 8, 8)
             back = lax.rem(span - lax.rem(place, 8), span)
-            flag = jnp.where(r < count_ref[head], 1.0, 0.0)
+            flag = jnp.where(r < slots_ref[head], 1.0, 0.0)
             for y in range(side):
                 line = pltpu.roll(ext[top + y, pl.ds(base, span), :], back, 0)[:wide]
                 line = jnp.where(inside, line, 0.0)
@@ -70,7 +69,7 @@
 
 
 def conv_kernel(n, cap, boxes, side, wide, me_ref, own_ref, got_ref, weight_ref, up_ref,
-                back_own, back_send, terms_ref, slots, shift, x3, s3, sl, cg, picks):
+                back_own, back_send, x3, sl, slots, shift, s3, cg, picks):
     channels = weight_ref.shape[2]
     area, full = side * wide, (side + 2) * wide
     me = me_ref[0]
@@ -133,6 +132,10 @@
                 back_own[r] = back.astype(jnp.bfloat16)
             else:
                 back_send[k - 1, r] = back.astype(jnp.bfloat16)
+
+
+def terms_kernel(boxes, side, wide, x3, sl, terms_ref):
+    channels, area = sl.shape[2], side * wide
     for a in range(3):
         total = jnp.zeros((3 * channels, channels), jnp.float32)
         for b in range(boxes):
@@ -146,7 +149,7 @@
             terms_ref[start : start + depth, :] = total[:, h * LANES : (h + 1) * LANES]
 
 
-def paste_kernel(n, cap, side, wide, me_ref, count_ref, row_ref, col_ref, own_ref, got_ref, main_ref, spill_ref, canvas):
+def paste_kernel(n, cap, side, wide, me_ref, slots_ref, own_ref, got_ref, main_ref, spill_ref, canvas):
     height, width = main_ref.shape[0], main_ref.shape[1]
     canvas[...] = jnp.zeros_like(canvas)
     me = me_ref[0]
@@ -154,9 +157,9 @@
         head = lax.rem(me + k, n)
         for r in range(cap):
 
-            @pl.when(r < count_ref[head])
+            @pl.when(r < slots_ref[head])
             def _():
-                top, place = row_ref[head * cap + r], col_ref[head * cap + r] + EDGE - 1
+                top, place = slots_ref[n + head * cap + r], slots_ref[n + (n + head) * cap + r] + EDGE - 1
                 base = pl.multiple_of(place // 8 * 8, 8)
                 ahead = lax.rem(place, 8)
                 for y in range(side):
@@ -192,11 +195,13 @@
     if len(far) % 2 == 0:
         far = [(name, bit, 4) for name, bit, _ in far[::2]]
     unit = 16 * 32
-    top = -(-(rows // unit) // 2) * unit
-    return [
-        (0, part_steps(first + second + head_bits + far, top)),
-        (top, part_steps(first + head_bits + second + far, rows - top)),
-    ]
+    parts, begin, pieces = [], 0, 4
+    for at in range(pieces):
+        size = ((rows // unit) // pieces + (at < (rows // unit) % pieces)) * unit
+        near = second + head_bits if at % 2 == 0 else head_bits + second
+        parts.append((begin, part_steps(first + near + far, size)))
+        begin += size
+    return parts
 
 
 def peer(name, stride, radix, hop):
@@ -273,7 +278,7 @@
             copy.wait()
 
 
-def reduce_kernel(parts, layout, terms_ref, out_ref, total, whole, send_sem, recv_sem, *bufs):
+def reduce_kernel(parts, layout, terms_ref, after_ref, out_ref, total, whole, send_sem, recv_sem, *bufs):
     greet(parts)
     walks = []
     for at, (begin, steps) in enumerate(parts):
@@ -286,7 +291,7 @@
     out_ref[...] = whole[...]
 
 
-def reduced(terms, tiles, heads):
+def reduced(terms, after, tiles, heads):
     rows = terms.shape[0]
     parts = plan(tiles, heads, rows)
     bufs, layout, wires = [], [], 0
@@ -305,7 +310,7 @@
     return pl.pallas_call(
         functools.partial(reduce_kernel, parts, layout),
         out_shape=jax.ShapeDtypeStruct((rows, LANES), jnp.bfloat16),
-        in_specs=[VM],
+        in_specs=[VM, pl.BlockSpec(memory_space=pl.ANY)],
         out_specs=VM,
         scratch_shapes=[
             pltpu.VMEM(terms.shape, jnp.float32),
@@ -319,7 +324,7 @@
         ),
         cost_estimate=pl.CostEstimate(flops=10**6, bytes_accessed=100 * 10**6, transcendentals=0),
         name="term_sum",
-    )(terms)
+    )(terms, after)
 
 
 def on_device(feature_map, weight, mask_grad, send_count, send_row, send_col):
@@ -333,20 +338,19 @@
     others = max(n - 1, 1)
     below = shifted(tile_map[:halo], "tile", -1)
     me = lax.axis_index("dp").reshape(1)
-    counts = send_count.reshape(-1)
-    tops, lefts = send_row.reshape(-1), send_col.reshape(-1)
+    slots = jnp.concatenate([send_count.reshape(-1), send_row.reshape(-1), send_col.reshape(-1)])
     room = EDGE + width + 2 * EDGE
     own_shape = jax.ShapeDtypeStruct((cap, side, wide, channels), jnp.bfloat16)
     send_shape = jax.ShapeDtypeStruct((others, cap, side, wide, channels), jnp.bfloat16)
     own, send = pl.pallas_call(
         functools.partial(cut_kernel, n, cap, side, wide),
         out_shape=(own_shape, send_shape),
-        in_specs=[SM, SM, SM, SM, VM, VM],
+        in_specs=[SM, SM, VM, VM],
         out_specs=(VM, VM),
         scratch_shapes=[pltpu.VMEM((height + halo, room, channels), jnp.float32)],
         compiler_params=LOCAL,
         name="cut",
-    )(me, counts, tops, lefts, tile_map, below)
+    )(me, slots, tile_map, below)
 
     def swapped(array, sign):
         parts = [rotated(array[k - 1], "dp", sign * k) for k in range(1, n)]
@@ -356,17 +360,20 @@
     upstream = jnp.pad(mask_grad[0, 0], ((0, 0), (0, 0), (1, wide - side - 1), (0, 0)))
     full = (side + 2) * wide
     rows = 9 * channels * (channels // LANES)
-    back_own, back_send, terms = pl.pallas_call(
+    back_own, back_send, x3, slopes = pl.pallas_call(
         functools.partial(conv_kernel, n, cap, boxes, side, wide),
-        out_shape=(own_shape, send_shape, jax.ShapeDtypeStruct((rows, LANES), jnp.float32)),
+        out_shape=(
+            own_shape,
+            send_shape,
+            jax.ShapeDtypeStruct((boxes, full, 3 * channels), jnp.bfloat16),
+            jax.ShapeDtypeStruct((boxes, side * wide, channels), jnp.bfloat16),
+        ),
         in_specs=[SM, VM, VM, VM, VM],
-        out_specs=(VM, VM, VM),
+        out_specs=(VM, VM, VM, VM),
         scratch_shapes=[
             pltpu.VMEM((n, cap, side, wide, channels), jnp.bfloat16),
             pltpu.VMEM((full + 2 * EDGE, channels), jnp.float32),
             pltpu.VMEM((boxes, full, 3 * channels), jnp.bfloat16),
-            pltpu.VMEM((boxes, full, 3 * channels), jnp.bfloat16),
-            pltpu.VMEM((boxes, side * wide, channels), jnp.bfloat16),
             pltpu.VMEM((boxes, side, wide, channels), jnp.bfloat16),
             pltpu.VMEM((boxes, n * cap, 1, channels), jnp.float32),
         ],
@@ -374,21 +381,32 @@
         name="conv",
     )(me, own, got, weight, upstream)
     back_got = swapped(back_send, -1)
-    whole = reduced(terms, tiles, heads)
+    terms = pl.pallas_call(
+        functools.partial(terms_kernel, boxes, side, wide),
+        out_shape=jax.ShapeDtypeStruct((rows, LANES), jnp.float32),
+        in_specs=[VM, VM],
+        out_specs=VM,
+        compiler_params=LOCAL,
+        cost_estimate=pl.CostEstimate(
+            flops=18 * boxes * side * wide * channels * channels, bytes_accessed=6 * 10**6, transcendentals=0
+        ),
+        name="terms",
+    )(x3, slopes)
     main, spill = pl.pallas_call(
         functools.partial(paste_kernel, n, cap, side, wide),
         out_shape=(
             jax.ShapeDtypeStruct((height, width, channels), jnp.float32),
             jax.ShapeDtypeStruct((halo, width, channels), jnp.bfloat16),
         ),
-        in_specs=[SM, SM, SM, SM, VM, VM],
+        in_specs=[SM, SM, VM, VM],
         out_specs=(VM, VM),
         scratch_shapes=[pltpu.VMEM((height + halo, room, channels), jnp.float32)],
         compiler_params=LOCAL,
         name="paste",
-    )(me, counts, tops, lefts, back_own, back_got)
+    )(me, slots, back_own, back_got)
     arriving = shifted(spill, "tile", 1)
-    map_grad = main.at[:halo].add(arriving.astype(jnp.float32))
+    whole = reduced(terms, spill, tiles, heads)
+    map_grad = jnp.concatenate([main[:halo] + arriving.astype(jnp.float32), main[halo:]], 0)
     box_total = boxes * tiles * heads
     halves = whole.reshape(channels // LANES, 9 * channels, LANES)
     summed = jnp.concatenate([halves[h] for h in range(channels // LANES)], -1)

time: 70.7 us -> 70.8 us (level)
  the two profiles are of different devices: /device:TPU:8 before, /device:TPU:0 now
where the time goes in v3:
time: 70.8 us; the launch traced here: 70.4 us
  Pallas kernels  42.7 us (60%)
  starting transfers between devices  12.5 us (18%)
  waiting for transfers between devices  6.23 us (9%)
  local copies, waits for them, and re-layouts  4.72 us (7%)
  other arithmetic  3.57 us (5%)
  between operations  0.73 us (1%)
    pallas_call x1, Pallas kernels, reduced(): pl.pallas_call(functools.partial(reduce_kernel, parts, layout), out_shape...  37.3 us
    ppermute x2, starting transfers between devices, shifted(): return lax.ppermute(array, axis, pairs)  7.37 us
    ppermute x2, waiting for transfers between devices, rotated(): lax.ppermute(array, axis, [(i, (i + by) % length) for i in range(length)])  6.12 us
    ppermute x2, starting transfers between devices, rotated(): lax.ppermute(array, axis, [(i, (i + by) % length) for i in range(length)])  5.12 us
    pallas_call x1, Pallas kernels, on_device(): pl.pallas_call(functools.partial(conv_kernel, n, cap, boxes, side, wide),...  2.51 us
    unnamed x5, local copies, waits for them, and re-layouts  2 us
    div x1, other arithmetic, on_device(): summed.reshape(9, channels, channels).astype(jnp.float32) / box_total  1.66 us
  transfers between devices with their start and end apart: 4, of which 3 were waited for; matrix products, arithmetic and copies ran while one was open for 7% of the time, Pallas kernels for 54%

profile of v3, /device:TPU:0, one launch (start us, length us, event | category | flops | bytes accessed | tf_op | source)
XLA Modules:
  0.0 70.4 jit_solution(18390619050055410734)
XLA Ops:
  0.6 1.0 %slice_bitcast_fusion = bf16[13,64,256]{2,1,0:T(8,128)(2,1)S(1)} fusion(bf16[1,16,64,256]{3,2,1,0:T(8,128)(2,1)} %param.6), kind=kLoop, calls=%fused_computation.3 | loop fusion | bytes 851968 | tf_op jit(solution)/shard_map/slice | solution.py:339
  1.7 1.3 %collective-permute-start = (bf16[13,64,256]{2,1,0:T(8,128)(2,1)S(1)}, bf16[13,64,256]{2,1,0:T(8,128)(2,1)S(1)}, u32[]{:S(2)}, u32[]{:S(2)}) collective-permute-start(bf16[13,64,256]{2,1,0:T(8,128)(2,1)S(1)} %slice_bitcast_fusion), channel_id=1, source_target_pairs={{2,0},{4,2},{6,4},{8,6},{10,8},{12,10},{14,12},{16,14},{18,16},{20... | collective-permute-start | bytes 1277960 | tf_op jit(solution)/shard_map/ppermute | solution.py:23
  3.0 0.8 %reshape.27 = s32[4]{0:T(128)S(1)} reshape(s32[1,1,2,2]{3,2,1,0:T(2,128)} %param.10) | data formatting | bytes 32 | tf_op jit(solution)/shard_map/reshape | solution.py:341
  3.7 0.8 %reshape.28 = s32[4]{0:T(128)S(1)} reshape(s32[1,1,2,2]{3,2,1,0:T(2,128)} %param.11) | data formatting | bytes 32 | tf_op jit(solution)/shard_map/reshape | solution.py:341
  4.5 0.7 %pad_add_fusion.slots_ref = s32[10]{0:T(128)S(1)} fusion(s32[4]{0:T(128)S(1)} %reshape.28, s32[4]{0:T(128)S(1)} %reshape.27, s32[2]{0:T(128)} %bitcast.24), kind=kLoop, calls=%fused_computation.5 | loop fusion | flops 20 | bytes 80 | tf_op jit(solution)/shard_map/concatenate | solution.py:341
  5.2 0.1 collective-permute-done.below_ref
  5.3 0.0 copy-start
  5.3 1.0 %copy-done = bf16[1,16,64,256]{3,2,1,0:T(8,128)(2,1)S(1)} copy-done((bf16[1,16,64,256]{3,2,1,0:T(8,128)(2,1)S(1)}, bf16[1,16,64,256]{3,2,1,0:T(8,128)(2,1)}, u32[]{:S(2)}) %copy-start) | copy-done | bytes 524312
  6.4 0.0 copy-start.1
  6.4 0.9 %cut.1 = (bf16[2,14,16,256]{3,2,1,0:T(8,128)(2,1)S(1)}, bf16[1,2,14,16,256]{4,3,2,1,0:T(8,128)(2,1)S(1)}) custom-call(s32[1]{0:T(128)} %bitcast.me_ref, s32[10]{0:T(128)S(1)} %pad_add_fusion.slots_ref, bf16[16,64,256]{2,1,0:T(8,128)(2,1)S(1)} %bitcast.16, bf16[13,64,256]{2,1,0:T(8,128)(2,1)S(1)} %collective-permute-done.below_ref), custom_call_target="tpu_custom_call" | custom-call | tf_op jit(solution)/shard_map/cut/pallas_call | solution.py:345
  7.3 3.0 %collective-permute-start.1 = (bf16[2,14,16,256]{3,2,1,0:T(8,128)(2,1)S(1)}, bf16[2,14,16,256]{3,2,1,0:T(8,128)(2,1)S(1)}, u32[]{:S(2)}, u32[]{:S(2)}) collective-permute-start(bf16[2,14,16,256]{3,2,1,0:T(8,128)(2,1)S(1)} %bitcast.20), channel_id=1, source_target_pairs={{0,1},{1,0},{2,3},{3,2},{4,5},{5,4},{6,7},{7,6},{8,9},{9,8},{10,11... | collective-permute-start | bytes 688136 | tf_op jit(solution)/shard_map/ppermute | solution.py:28
  10.3 1.0 %copy.10 = bf16[1,1,2,14,14,256]{5,4,3,2,1,0:T(8,128)(2,1)S(1)} copy(bf16[1,1,2,14,14,256]{5,2,4,3,1,0:T(2,128)(2,1)} %param.8) | data formatting | bytes 401408 | tf_op args[2]
  11.3 0.1 pad.4.up_ref
  11.4 3.0 %collective-permute-done.1 = bf16[2,14,16,256]{3,2,1,0:T(8,128)(2,1)S(1)} collective-permute-done((bf16[2,14,16,256]{3,2,1,0:T(8,128)(2,1)S(1)}, bf16[2,14,16,256]{3,2,1,0:T(8,128)(2,1)S(1)}, u32[]{:S(2)}, u32[]{:S(2)}) %collective-permute-start.1) | collective-permute-done | bytes 229408 | tf_op jit(solution)/shard_map/ppermute | solution.py:28
  14.3 0.0 copy-done.1
  14.3 2.5 %conv.1 = (bf16[2,14,16,256]{3,2,1,0:T(8,128)(2,1)S(1)}, bf16[1,2,14,16,256]{4,3,2,1,0:T(8,128)(2,1)S(1)}, bf16[2,256,768]{2,1,0:T(8,128)(2,1)S(1)}, bf16[2,224,256]{2,1,0:T(8,128)(2,1)S(1)}) custom-call(s32[1]{0:T(128)} %bitcast.me_ref, bf16[2,14,16,256]{3,2,1,0:T(8,128)(2,1)S(1)} %get-tuple-element.10.own_ref, bf16[1,2,14,16,256]{4,3,2,1,0:T(8,128)(2,1)S(1)} %bitcast.18, ...), custom_call_target="tpu_custom_call" | custom-call | tf_op jit(solution)/shard_map/conv/pallas_call | solution.py:363
  16.9 2.1 %collective-permute-start.2 = (bf16[2,14,16,256]{3,2,1,0:T(8,128)(2,1)S(1)}, bf16[2,14,16,256]{3,2,1,0:T(8,128)(2,1)S(1)}, u32[]{:S(2)}, u32[]{:S(2)}) collective-permute-start(bf16[2,14,16,256]{3,2,1,0:T(8,128)(2,1)S(1)} %bitcast.19), channel_id=1, source_target_pairs={{0,1},{1,0},{2,3},{3,2},{4,5},{5,4},{6,7},{7,6},{8,9},{9,8},{10,11... | collective-permute-start | bytes 688136 | tf_op jit(solution)/shard_map/ppermute | solution.py:28
  19.0 0.8 %terms.1.terms_ref = f32[4608,128]{1,0:T(8,128)S(1)} custom-call(bf16[2,256,768]{2,1,0:T(8,128)(2,1)S(1)} %get-tuple-element.16.x3, bf16[2,224,256]{2,1,0:T(8,128)(2,1)S(1)} %get-tuple-element.17.sl), custom_call_target="tpu_custom_call" | custom-call | flops 528482304 | bytes 6000000 | tf_op jit(solution)/shard_map/terms/pallas_call | solution.py:384
  19.8 3.2 %collective-permute-done.2 = bf16[2,14,16,256]{3,2,1,0:T(8,128)(2,1)S(1)} collective-permute-done((bf16[2,14,16,256]{3,2,1,0:T(8,128)(2,1)S(1)}, bf16[2,14,16,256]{3,2,1,0:T(8,128)(2,1)S(1)}, u32[]{:S(2)}, u32[]{:S(2)}) %collective-permute-start.2) | collective-permute-done | bytes 229408 | tf_op jit(solution)/shard_map/ppermute | solution.py:28
  23.0 1.2 %paste.1 = (f32[16,64,256]{2,1,0:T(8,128)S(1)}, bf16[13,64,256]{2,1,0:T(8,128)(2,1)S(1)}) custom-call(s32[1]{0:T(128)} %bitcast.me_ref, s32[10]{0:T(128)S(1)} %pad_add_fusion.slots_ref, bf16[2,14,16,256]{3,2,1,0:T(8,128)(2,1)S(1)} %get-tuple-element.12.own_ref, bf16[1,2,14,16,256]{4,3,2,1,0:T(8,128)(2,1)S(1)} %bitcast.17), custom_call_target="tpu_custom_call" | custom-call | tf_op jit(solution)/shard_map/paste/pallas_call | solution.py:395
  24.1 6.1 %collective-permute-start.3 = (bf16[13,64,256]{2,1,0:T(8,128)(2,1)S(1)}, bf16[13,64,256]{2,1,0:T(8,128)(2,1)S(1)}, u32[]{:S(2)}, u32[]{:S(2)}) collective-permute-start(bf16[13,64,256]{2,1,0:T(8,128)(2,1)S(1)} %get-tuple-element.15.after_ref), channel_id=1, source_target_pairs={{0,2},{2,4},{4,6},{6,8},{8,10},{10,12},{12,14},{14,16},{16,18},{18... | collective-permute-start | bytes 1277960 | tf_op jit(solution)/shard_map/ppermute | solution.py:23
  30.2 37.3 %term_sum.1 = bf16[4608,128]{1,0:T(8,128)(2,1)S(1)} custom-call(f32[4608,128]{1,0:T(8,128)S(1)} %terms.1.terms_ref, bf16[13,64,256]{2,1,0:T(8,128)(2,1)S(1)} %get-tuple-element.15.after_ref), custom_call_target="tpu_custom_call" | custom-call | flops 1000000 | bytes 100000000 | tf_op jit(solution)/shard_map/term_sum/pallas_call | solution.py:310
  67.5 0.1 fusion
  67.6 1.7 %convert_multiply_fusion = f32[9,256,256]{2,1,0:T(8,128)} fusion(bf16[9,256,128]{2,1,0:T(8,128)(2,1)S(1)} %bitcast.22, bf16[9,256,128]{2,1,0:T(8,128)(2,1)S(1)} %bitcast.21), kind=kLoop, calls=%fused_computation | loop fusion | flops 2949120 | bytes 3538944 | tf_op jit(solution)/shard_map/div | solution.py:413
  69.3 0.0 collective-permute-done.3
  69.3 0.1 convert_add_fusion
  69.4 1.1 %maximum_bitcast_fusion = f32[1,16,64,256]{3,2,1,0:T(8,128)} fusion(f32[3,64,256]{2,1,0:T(8,128)S(1)} %slice.23, f32[13,64,256]{2,1,0:T(8,128)S(1)} %convert_add_fusion), kind=kLoop, calls=%fused_computation.1 | loop fusion | flops 262144 | bytes 2097152 | tf_op jit(solution)/shard_map/broadcast_in_dim | solution.py:414
  (1 shorter events, 0.0 us)
Async XLA Ops:
  1.7 3.7 %collective-permute-start = (bf16[13,64,256]{2,1,0:T(8,128)(2,1)S(1)}, bf16[13,64,256]{2,1,0:T(8,128)(2,1)S(1)}, u32[]{:S(2)}, u32[]{:S(2)}) collective-permute-start(bf16[13,64,256]{2,1,0:T(8,128)(2,1)S(1)} %slice_bitcast_fusion), channel_id=1, source_target_pairs={{2,0},{4,2},{6,4},{8,6},{10,8},{12,10},{14,12},{16,14},{18,16},{20... | collective-permute-start | bytes 1277960 | tf_op jit(solution)/shard_map/ppermute | solution.py:23
  5.3 1.0 %copy-start = (bf16[1,16,64,256]{3,2,1,0:T(8,128)(2,1)S(1)}, bf16[1,16,64,256]{3,2,1,0:T(8,128)(2,1)}, u32[]{:S(2)}) copy-start(bf16[1,16,64,256]{3,2,1,0:T(8,128)(2,1)} %param.6) | copy-start | bytes 1572868
  6.4 8.0 %copy-start.1 = (bf16[9,256,256]{2,1,0:T(8,128)(2,1)S(1)}, bf16[9,256,256]{2,1,0:T(8,128)(2,1)}, u32[]{:S(2)}) copy-start(bf16[9,256,256]{2,1,0:T(8,128)(2,1)} %weight_ref.1) | copy-start | bytes 3538948
  7.3 7.0 %collective-permute-start.1 = (bf16[2,14,16,256]{3,2,1,0:T(8,128)(2,1)S(1)}, bf16[2,14,16,256]{3,2,1,0:T(8,128)(2,1)S(1)}, u32[]{:S(2)}, u32[]{:S(2)}) collective-permute-start(bf16[2,14,16,256]{3,2,1,0:T(8,128)(2,1)S(1)} %bitcast.20), channel_id=1, source_target_pairs={{0,1},{1,0},{2,3},{3,2},{4,5},{5,4},{6,7},{7,6},{8,9},{9,8},{10,11... | collective-permute-start | bytes 688136 | tf_op jit(solution)/shard_map/ppermute | solution.py:28
  16.9 6.1 %collective-permute-start.2 = (bf16[2,14,16,256]{3,2,1,0:T(8,128)(2,1)S(1)}, bf16[2,14,16,256]{3,2,1,0:T(8,128)(2,1)S(1)}, u32[]{:S(2)}, u32[]{:S(2)}) collective-permute-start(bf16[2,14,16,256]{3,2,1,0:T(8,128)(2,1)S(1)} %bitcast.19), channel_id=1, source_target_pairs={{0,1},{1,0},{2,3},{3,2},{4,5},{5,4},{6,7},{7,6},{8,9},{9,8},{10,11... | collective-permute-start | bytes 688136 | tf_op jit(solution)/shard_map/ppermute | solution.py:28
  24.1 45.1 %collective-permute-start.3 = (bf16[13,64,256]{2,1,0:T(8,128)(2,1)S(1)}, bf16[13,64,256]{2,1,0:T(8,128)(2,1)S(1)}, u32[]{:S(2)}, u32[]{:S(2)}) collective-permute-start(bf16[13,64,256]{2,1,0:T(8,128)(2,1)S(1)} %get-tuple-element.15.after_ref), channel_id=1, source_target_pairs={{0,2},{2,4},{4,6},{6,8},{8,10},{10,12},{12,14},{14,16},{16,18},{18... | collective-permute-start | bytes 1277960 | tf_op jit(solution)/shard_map/ppermute | solution.py:23

commit v4 on v3

--- a/solution.py
+++ b/solution.py
@@ -225,33 +225,29 @@
     pl.semaphore_wait(barrier, count)
 
 
-def walk(part_at, begin, steps, landings, stages, terms_ref, total, whole, send_sem, recv_sem):
+def send_to(source, target, device, sems, part_at, wire):
+    copy = pltpu.make_async_remote_copy(
+        src_ref=source, dst_ref=target, send_sem=sems[0].at[part_at, wire], recv_sem=sems[1].at[part_at, wire],
+        device_id=device, device_id_type=pl.DeviceIdType.MESH,
+    )
+    copy.start()
+    return copy
+
+
+def scatter_walk(part_at, begin, steps, landings, stages, terms_ref, total, out_ref, out_at, sems):
     base, wire = begin, 0
-    bases = [begin]
-
-    def copy_to(source, target, device):
-        nonlocal wire
-        copy = pltpu.make_async_remote_copy(
-            src_ref=source, dst_ref=target, send_sem=send_sem.at[part_at, wire], recv_sem=recv_sem.at[part_at, wire],
-            device_id=device, device_id_type=pl.DeviceIdType.MESH,
-        )
-        wire += 1
-        copy.start()
-        return copy
-
     for index, (name, stride, radix, halves, size) in enumerate(steps):
         held = terms_ref if index == 0 else total
         copies = []
         for hop in range(1, radix):
             digit, other, device = peer(name, stride, radix, hop)
             give = pl.multiple_of(base + other * size, 16) if halves else base
-            landing = landings[index].at[hop - 1]
+            source = held.at[pl.ds(give, size), :]
             if halves and index > 0:
-                stage = stages[index].at[hop - 1]
-                stage[...] = held[pl.ds(give, size), :].astype(jnp.bfloat16)
-                copies.append(copy_to(stage, landing, device))
-            else:
-                copies.append(copy_to(held.at[pl.ds(give, size), :], landing, device))
+                stages[index][hop - 1] = held[pl.ds(give, size), :].astype(jnp.bfloat16)
+                source = stages[index].at[hop - 1]
+            copies.append(send_to(source, landings[index].at[hop - 1], device, sems, part_at, wire))
+            wire += 1
         yield
         keep = pl.multiple_of(base + digit * size, 16) if halves else base
         for copy in copies:
@@ -260,41 +256,70 @@
         for hop in range(1, radix):
             value = value + landings[index][hop - 1].astype(jnp.float32)
         if index == len(steps) - 1:
-            whole[pl.ds(keep, size), :] = value.astype(jnp.bfloat16)
+            out_ref[out_at : out_at + size, :] = value.astype(jnp.bfloat16)
         else:
             total[pl.ds(keep, size), :] = value
-        if halves:
-            bases.append(keep)
         base = keep
+
+
+def gather_walk(part_at, begin, steps, part_ref, part_row, whole, sems):
     halving = [step for step in steps if step[3]]
+    bases, wire = [begin], 0
+    for name, stride, radix, _, size in halving:
+        bases.append(pl.multiple_of(bases[-1] + peer(name, stride, radix, 1)[0] * size, 16))
+    last = halving[-1][4]
+    whole[pl.ds(bases[-1], last), :] = part_ref[part_row : part_row + last, :]
     for index in reversed(range(len(halving))):
         name, stride, radix, _, size = halving[index]
         mine = whole.at[pl.ds(bases[index + 1], size), :]
-        copies = [
-            copy_to(mine, mine, peer(name, stride, radix, hop)[2]) for hop in range(1, radix)
-        ]
+        copies = []
+        for hop in range(1, radix):
+            copies.append(send_to(mine, mine, peer(name, stride, radix, hop)[2], sems, part_at, wire))
+            wire += 1
         yield
         for copy in copies:
             copy.wait()
 
 
-def reduce_kernel(parts, layout, terms_ref, after_ref, out_ref, total, whole, send_sem, recv_sem, *bufs):
+def part_rows(parts):
+    sizes = [steps[-1][4] for _, steps in parts]
+    return [sum(sizes[:at]) for at in range(len(sizes) + 1)]
+
+
+def run(walks):
+    while walks:
+        walks = [w for w in walks if next(w, 0) is None]
+
+
+def scatter_kernel(parts, layout, terms_ref, out_ref, total, send_sem, recv_sem, *bufs):
     greet(parts)
-    walks = []
+    places, walks = part_rows(parts), []
     for at, (begin, steps) in enumerate(parts):
         landings, stages = [[bufs[i] if i is not None else None for i in row] for row in layout[at]]
         walks.append(
-            walk(at, begin, steps, landings, stages, terms_ref, total, whole, send_sem, recv_sem)
+            scatter_walk(at, begin, steps, landings, stages, terms_ref, total, out_ref, places[at], (send_sem, recv_sem))
         )
-    while walks:
-        walks = [w for w in walks if next(w, 0) is None]
+    run(walks)
+
+
+def gather_kernel(parts, part_ref, after_ref, out_ref, whole, send_sem, recv_sem):
+    greet([(begin, [step for step in steps if step[3]]) for begin, steps in parts])
+    places = part_rows(parts)
+    run([
+        gather_walk(at, begin, steps, part_ref, places[at], whole, (send_sem, recv_sem))
+        for at, (begin, steps) in enumerate(parts)
+    ])
     out_ref[...] = whole[...]
 
 
-def reduced(terms, after, tiles, heads):
-    rows = terms.shape[0]
-    parts = plan(tiles, heads, rows)
-    bufs, layout, wires = [], [], 0
+def wire_sems(parts):
+    wires = max(sum(step[2] - 1 for step in steps) for _, steps in parts)
+    return [pltpu.SemaphoreType.DMA((len(parts), wires)) for _ in range(2)]
+
+
+def scattered(terms, tiles, heads):
+    parts = plan(tiles, heads, terms.shape[0])
+    bufs, layout = [], []
     for _, steps in parts:
         landings, stages = [], []
         for index, (_, _, radix, halves, size) in enumerate(steps):
@@ -306,25 +331,34 @@
             if narrow:
                 bufs.append(pltpu.VMEM(shape, jnp.bfloat16))
         layout.append((landings, stages))
-        wires = max(wires, sum(s[2] - 1 for s in steps) + sum(s[2] - 1 for s in steps if s[3]))
     return pl.pallas_call(
-        functools.partial(reduce_kernel, parts, layout),
+        functools.partial(scatter_kernel, parts, layout),
+        out_shape=jax.ShapeDtypeStruct((part_rows(parts)[-1], LANES), jnp.bfloat16),
+        in_specs=[VM],
+        out_specs=VM,
+        scratch_shapes=[pltpu.VMEM(terms.shape, jnp.float32), *wire_sems(parts), *bufs],
+        compiler_params=pltpu.CompilerParams(
+            collective_id=0, has_side_effects=True, vmem_limit_bytes=VMEM_BYTES
+        ),
+        cost_estimate=pl.CostEstimate(flops=10**6, bytes_accessed=50 * 10**6, transcendentals=0),
+        name="term_scatter",
+    )(terms)
+
+
+def gathered(part, after, tiles, heads, rows):
+    parts = plan(tiles, heads, rows)
+    return pl.pallas_call(
+        functools.partial(gather_kernel, parts),
         out_shape=jax.ShapeDtypeStruct((rows, LANES), jnp.bfloat16),
         in_specs=[VM, pl.BlockSpec(memory_space=pl.ANY)],
         out_specs=VM,
-        scratch_shapes=[
-            pltpu.VMEM(terms.shape, jnp.float32),
-            pltpu.VMEM(terms.shape, jnp.bfloat16),
-            pltpu.SemaphoreType.DMA((len(parts), wires)),
-            pltpu.SemaphoreType.DMA((len(parts), wires)),
-            *bufs,
-        ],
+        scratch_shapes=[pltpu.VMEM((rows, LANES), jnp.bfloat16), *wire_sems(parts)],
         compiler_params=pltpu.CompilerParams(
-            collective_id=0, has_side_effects=True, vmem_limit_bytes=VMEM_BYTES
+            collective_id=1, has_side_effects=True, vmem_limit_bytes=VMEM_BYTES
         ),
-        cost_estimate=pl.CostEstimate(flops=10**6, bytes_accessed=100 * 10**6, transcendentals=0),
-        name="term_sum",
-    )(terms, after)
+        cost_estimate=pl.CostEstimate(flops=10**6, bytes_accessed=50 * 10**6, transcendentals=0),
+        name="term_gather",
+    )(part, after)
 
 
 def on_device(feature_map, weight, mask_grad, send_count, send_row, send_col):
@@ -392,6 +426,7 @@
         ),
         name="terms",
     )(x3, slopes)
+    part = scattered(terms, tiles, heads)
     main, spill = pl.pallas_call(
         functools.partial(paste_kernel, n, cap, side, wide),
         out_shape=(
@@ -405,7 +440,7 @@
         name="paste",
     )(me, slots, back_own, back_got)
     arriving = shifted(spill, "tile", 1)
-    whole = reduced(terms, spill, tiles, heads)
+    whole = gathered(part, spill, tiles, heads, rows)
     map_grad = jnp.concatenate([main[:halo] + arriving.astype(jnp.float32), main[halo:]], 0)
     box_total = boxes * tiles * heads
     halves = whole.reshape(channels // LANES, 9 * channels, LANES)

time: 70.8 us -> 67.2 us (0.949)
  Pallas kernels: 42.7 us -> 47.5 us
  starting transfers between devices: 12.5 us -> 7.73 us
  waiting for transfers between devices: 6.23 us -> 3.08 us
    pallas_call x1 -> x2, Pallas kernels: 37.3 us -> 42.1 us  [the longest x1 24 us: scattered(): pl.pallas_call(functools.partial(scatter_kernel, parts, layout), out_shap...]
    ppermute x2, starting transfers between devices: 7.37 us -> 2.61 us  [shifted(): return lax.ppermute(array, axis, pairs)]
    ppermute x2, waiting for transfers between devices: 6.12 us -> 2.97 us  [rotated(): lax.ppermute(array, axis, [(i, (i + by) % length) for i in range(length)])]
  transfers between devices with their start and end apart: 4 -> 4, of which waited for: 3 -> 2; matrix products, arithmetic and copies ran while one was open for 7% -> 7% of each run, Pallas kernels for 54% -> 64%
where the time goes in v4:
time: 67.2 us; the launch traced here: 67.3 us
  Pallas kernels  47.5 us (71%)
  starting transfers between devices  7.73 us (12%)
  local copies, waits for them, and re-layouts  4.72 us (7%)
  other arithmetic  3.55 us (5%)
  waiting for transfers between devices  3.08 us (5%)
  between operations  0.74 us (1%)
    pallas_call x1, Pallas kernels, scattered(): pl.pallas_call(functools.partial(scatter_kernel, parts, layout), out_shap...  24 us
    pallas_call x1, Pallas kernels, gathered(): pl.pallas_call(functools.partial(gather_kernel, parts), out_shape=jax.Sha...  18.1 us
    ppermute x2, starting transfers between devices, rotated(): lax.ppermute(array, axis, [(i, (i + by) % length) for i in range(length)])  5.12 us
    ppermute x2, waiting for transfers between devices, rotated(): lax.ppermute(array, axis, [(i, (i + by) % length) for i in range(length)])  2.97 us
    ppermute x2, starting transfers between devices, shifted(): return lax.ppermute(array, axis, pairs)  2.61 us
    pallas_call x1, Pallas kernels, on_device(): pl.pallas_call(functools.partial(conv_kernel, n, cap, boxes, side, wide),...  2.51 us
    unnamed x5, local copies, waits for them, and re-layouts  2 us
    div x1, other arithmetic, on_device(): summed.reshape(9, channels, channels).astype(jnp.float32) / box_total  1.66 us
  transfers between devices with their start and end apart: 4, of which 2 were waited for; matrix products, arithmetic and copies ran while one was open for 7% of the time, Pallas kernels for 64%

profile of v4, /device:TPU:0, one launch (start us, length us, event | category | flops | bytes accessed | tf_op | source)
XLA Modules:
  0.0 67.3 jit_solution(17099342001363753392)
XLA Ops:
  0.6 1.0 %slice_bitcast_fusion = bf16[13,64,256]{2,1,0:T(8,128)(2,1)S(1)} fusion(bf16[1,16,64,256]{3,2,1,0:T(8,128)(2,1)} %param.6), kind=kLoop, calls=%fused_computation.3 | loop fusion | bytes 851968 | tf_op jit(solution)/shard_map/slice | solution.py:373
  1.7 1.3 %collective-permute-start = (bf16[13,64,256]{2,1,0:T(8,128)(2,1)S(1)}, bf16[13,64,256]{2,1,0:T(8,128)(2,1)S(1)}, u32[]{:S(2)}, u32[]{:S(2)}) collective-permute-start(bf16[13,64,256]{2,1,0:T(8,128)(2,1)S(1)} %slice_bitcast_fusion), channel_id=1, source_target_pairs={{2,0},{4,2},{6,4},{8,6},{10,8},{12,10},{14,12},{16,14},{18,16},{20... | collective-permute-start | bytes 1277960 | tf_op jit(solution)/shard_map/ppermute | solution.py:23
  3.0 0.8 %reshape.27 = s32[4]{0:T(128)S(1)} reshape(s32[1,1,2,2]{3,2,1,0:T(2,128)} %param.10) | data formatting | bytes 32 | tf_op jit(solution)/shard_map/reshape | solution.py:375
  3.7 0.8 %reshape.28 = s32[4]{0:T(128)S(1)} reshape(s32[1,1,2,2]{3,2,1,0:T(2,128)} %param.11) | data formatting | bytes 32 | tf_op jit(solution)/shard_map/reshape | solution.py:375
  4.5 0.7 %pad_add_fusion.slots_ref = s32[10]{0:T(128)S(1)} fusion(s32[4]{0:T(128)S(1)} %reshape.28, s32[4]{0:T(128)S(1)} %reshape.27, s32[2]{0:T(128)} %bitcast.24), kind=kLoop, calls=%fused_computation.5 | loop fusion | flops 20 | bytes 80 | tf_op jit(solution)/shard_map/concatenate | solution.py:375
  5.2 0.1 collective-permute-done.below_ref
  5.3 0.0 copy-start
  5.3 1.0 %copy-done = bf16[1,16,64,256]{3,2,1,0:T(8,128)(2,1)S(1)} copy-done((bf16[1,16,64,256]{3,2,1,0:T(8,128)(2,1)S(1)}, bf16[1,16,64,256]{3,2,1,0:T(8,128)(2,1)}, u32[]{:S(2)}) %copy-start) | copy-done | bytes 524312
  6.4 0.0 copy-start.1
  6.4 0.9 %cut.1 = (bf16[2,14,16,256]{3,2,1,0:T(8,128)(2,1)S(1)}, bf16[1,2,14,16,256]{4,3,2,1,0:T(8,128)(2,1)S(1)}) custom-call(s32[1]{0:T(128)} %bitcast.me_ref, s32[10]{0:T(128)S(1)} %pad_add_fusion.slots_ref, bf16[16,64,256]{2,1,0:T(8,128)(2,1)S(1)} %bitcast.16, bf16[13,64,256]{2,1,0:T(8,128)(2,1)S(1)} %collective-permute-done.below_ref), custom_call_target="tpu_custom_call" | custom-call | tf_op jit(solution)/shard_map/cut/pallas_call | solution.py:379
  7.3 3.0 %collective-permute-start.1 = (bf16[2,14,16,256]{3,2,1,0:T(8,128)(2,1)S(1)}, bf16[2,14,16,256]{3,2,1,0:T(8,128)(2,1)S(1)}, u32[]{:S(2)}, u32[]{:S(2)}) collective-permute-start(bf16[2,14,16,256]{3,2,1,0:T(8,128)(2,1)S(1)} %bitcast.20), channel_id=1, source_target_pairs={{0,1},{1,0},{2,3},{3,2},{4,5},{5,4},{6,7},{7,6},{8,9},{9,8},{10,11... | collective-permute-start | bytes 688136 | tf_op jit(solution)/shard_map/ppermute | solution.py:28
  10.3 1.0 %copy.10 = bf16[1,1,2,14,14,256]{5,4,3,2,1,0:T(8,128)(2,1)S(1)} copy(bf16[1,1,2,14,14,256]{5,2,4,3,1,0:T(2,128)(2,1)} %param.8) | data formatting | bytes 401408 | tf_op args[2]
  11.3 0.1 pad.4.up_ref
  11.4 3.0 %collective-permute-done.1 = bf16[2,14,16,256]{3,2,1,0:T(8,128)(2,1)S(1)} collective-permute-done((bf16[2,14,16,256]{3,2,1,0:T(8,128)(2,1)S(1)}, bf16[2,14,16,256]{3,2,1,0:T(8,128)(2,1)S(1)}, u32[]{:S(2)}, u32[]{:S(2)}) %collective-permute-start.1) | collective-permute-done | bytes 229408 | tf_op jit(solution)/shard_map/ppermute | solution.py:28
  14.3 0.0 copy-done.1
  14.3 2.5 %conv.1 = (bf16[2,14,16,256]{3,2,1,0:T(8,128)(2,1)S(1)}, bf16[1,2,14,16,256]{4,3,2,1,0:T(8,128)(2,1)S(1)}, bf16[2,256,768]{2,1,0:T(8,128)(2,1)S(1)}, bf16[2,224,256]{2,1,0:T(8,128)(2,1)S(1)}) custom-call(s32[1]{0:T(128)} %bitcast.me_ref, bf16[2,14,16,256]{3,2,1,0:T(8,128)(2,1)S(1)} %get-tuple-element.10.own_ref, bf16[1,2,14,16,256]{4,3,2,1,0:T(8,128)(2,1)S(1)} %bitcast.18, ...), custom_call_target="tpu_custom_call" | custom-call | tf_op jit(solution)/shard_map/conv/pallas_call | solution.py:397
  16.9 2.1 %collective-permute-start.2 = (bf16[2,14,16,256]{3,2,1,0:T(8,128)(2,1)S(1)}, bf16[2,14,16,256]{3,2,1,0:T(8,128)(2,1)S(1)}, u32[]{:S(2)}, u32[]{:S(2)}) collective-permute-start(bf16[2,14,16,256]{3,2,1,0:T(8,128)(2,1)S(1)} %bitcast.19), channel_id=1, source_target_pairs={{0,1},{1,0},{2,3},{3,2},{4,5},{5,4},{6,7},{7,6},{8,9},{9,8},{10,11... | collective-permute-start | bytes 688136 | tf_op jit(solution)/shard_map/ppermute | solution.py:28
  19.0 0.8 %terms.1.terms_ref = f32[4608,128]{1,0:T(8,128)S(1)} custom-call(bf16[2,256,768]{2,1,0:T(8,128)(2,1)S(1)} %get-tuple-element.16.x3, bf16[2,224,256]{2,1,0:T(8,128)(2,1)S(1)} %get-tuple-element.17.sl), custom_call_target="tpu_custom_call" | custom-call | flops 528482304 | bytes 6000000 | tf_op jit(solution)/shard_map/terms/pallas_call | solution.py:418
  19.8 24.0 %term_scatter.1.part_ref = bf16[144,128]{1,0:T(8,128)(2,1)S(1)} custom-call(f32[4608,128]{1,0:T(8,128)S(1)} %terms.1.terms_ref), custom_call_target="tpu_custom_call" | custom-call | flops 1000000 | bytes 50000000 | tf_op jit(solution)/shard_map/term_scatter/pallas_call | solution.py:334
  43.8 0.0 collective-permute-done.2
  43.8 1.2 %paste.1 = (f32[16,64,256]{2,1,0:T(8,128)S(1)}, bf16[13,64,256]{2,1,0:T(8,128)(2,1)S(1)}) custom-call(s32[1]{0:T(128)} %bitcast.me_ref, s32[10]{0:T(128)S(1)} %pad_add_fusion.slots_ref, bf16[2,14,16,256]{3,2,1,0:T(8,128)(2,1)S(1)} %get-tuple-element.12.own_ref, bf16[1,2,14,16,256]{4,3,2,1,0:T(8,128)(2,1)S(1)} %bitcast.17), custom_call_target="tpu_custom_call" | custom-call | tf_op jit(solution)/shard_map/paste/pallas_call | solution.py:430
  45.0 1.3 %collective-permute-start.3 = (bf16[13,64,256]{2,1,0:T(8,128)(2,1)S(1)}, bf16[13,64,256]{2,1,0:T(8,128)(2,1)S(1)}, u32[]{:S(2)}, u32[]{:S(2)}) collective-permute-start(bf16[13,64,256]{2,1,0:T(8,128)(2,1)S(1)} %get-tuple-element.15.after_ref), channel_id=1, source_target_pairs={{0,2},{2,4},{4,6},{6,8},{8,10},{10,12},{12,14},{14,16},{16,18},{18... | collective-permute-start | bytes 1277960 | tf_op jit(solution)/shard_map/ppermute | solution.py:23
  46.3 18.1 %term_gather.1 = bf16[4608,128]{1,0:T(8,128)(2,1)S(1)} custom-call(bf16[144,128]{1,0:T(8,128)(2,1)S(1)} %term_scatter.1.part_ref, bf16[13,64,256]{2,1,0:T(8,128)(2,1)S(1)} %get-tuple-element.15.after_ref), custom_call_target="tpu_custom_call" | custom-call | flops 1000000 | bytes 50000000 | tf_op jit(solution)/shard_map/term_gather/pallas_call | solution.py:350
  64.4 0.1 fusion
  64.5 1.7 %convert_multiply_fusion = f32[9,256,256]{2,1,0:T(8,128)} fusion(bf16[9,256,128]{2,1,0:T(8,128)(2,1)S(1)} %bitcast.22, bf16[9,256,128]{2,1,0:T(8,128)(2,1)S(1)} %bitcast.21), kind=kLoop, calls=%fused_computation | loop fusion | flops 2949120 | bytes 3538944 | tf_op jit(solution)/shard_map/div | solution.py:448
  66.1 0.0 collective-permute-done.3
  66.2 0.1 convert_add_fusion
  66.3 1.1 %maximum_bitcast_fusion = f32[1,16,64,256]{3,2,1,0:T(8,128)} fusion(f32[3,64,256]{2,1,0:T(8,128)S(1)} %slice.23, f32[13,64,256]{2,1,0:T(8,128)S(1)} %convert_add_fusion), kind=kLoop, calls=%fused_computation.1 | loop fusion | flops 262144 | bytes 2097152 | tf_op jit(solution)/shard_map/broadcast_in_dim | solution.py:449
  (1 shorter events, 0.0 us)
Async XLA Ops:
  1.7 3.7 %collective-permute-start = (bf16[13,64,256]{2,1,0:T(8,128)(2,1)S(1)}, bf16[13,64,256]{2,1,0:T(8,128)(2,1)S(1)}, u32[]{:S(2)}, u32[]{:S(2)}) collective-permute-start(bf16[13,64,256]{2,1,0:T(8,128)(2,1)S(1)} %slice_bitcast_fusion), channel_id=1, source_target_pairs={{2,0},{4,2},{6,4},{8,6},{10,8},{12,10},{14,12},{16,14},{18,16},{20... | collective-permute-start | bytes 1277960 | tf_op jit(solution)/shard_map/ppermute | solution.py:23
  5.3 1.0 %copy-start = (bf16[1,16,64,256]{3,2,1,0:T(8,128)(2,1)S(1)}, bf16[1,16,64,256]{3,2,1,0:T(8,128)(2,1)}, u32[]{:S(2)}) copy-start(bf16[1,16,64,256]{3,2,1,0:T(8,128)(2,1)} %param.6) | copy-start | bytes 1572868
  6.4 8.0 %copy-start.1 = (bf16[9,256,256]{2,1,0:T(8,128)(2,1)S(1)}, bf16[9,256,256]{2,1,0:T(8,128)(2,1)}, u32[]{:S(2)}) copy-start(bf16[9,256,256]{2,1,0:T(8,128)(2,1)} %weight_ref.1) | copy-start | bytes 3538948
  7.3 7.0 %collective-permute-start.1 = (bf16[2,14,16,256]{3,2,1,0:T(8,128)(2,1)S(1)}, bf16[2,14,16,256]{3,2,1,0:T(8,128)(2,1)S(1)}, u32[]{:S(2)}, u32[]{:S(2)}) collective-permute-start(bf16[2,14,16,256]{3,2,1,0:T(8,128)(2,1)S(1)} %bitcast.20), channel_id=1, source_target_pairs={{0,1},{1,0},{2,3},{3,2},{4,5},{5,4},{6,7},{7,6},{8,9},{9,8},{10,11... | collective-permute-start | bytes 688136 | tf_op jit(solution)/shard_map/ppermute | solution.py:28
  16.9 26.9 %collective-permute-start.2 = (bf16[2,14,16,256]{3,2,1,0:T(8,128)(2,1)S(1)}, bf16[2,14,16,256]{3,2,1,0:T(8,128)(2,1)S(1)}, u32[]{:S(2)}, u32[]{:S(2)}) collective-permute-start(bf16[2,14,16,256]{3,2,1,0:T(8,128)(2,1)S(1)} %bitcast.19), channel_id=1, source_target_pairs={{0,1},{1,0},{2,3},{3,2},{4,5},{5,4},{6,7},{7,6},{8,9},{9,8},{10,11... | collective-permute-start | bytes 688136 | tf_op jit(solution)/shard_map/ppermute | solution.py:28
  45.0 21.2 %collective-permute-start.3 = (bf16[13,64,256]{2,1,0:T(8,128)(2,1)S(1)}, bf16[13,64,256]{2,1,0:T(8,128)(2,1)S(1)}, u32[]{:S(2)}, u32[]{:S(2)}) collective-permute-start(bf16[13,64,256]{2,1,0:T(8,128)(2,1)S(1)} %get-tuple-element.15.after_ref), channel_id=1, source_target_pairs={{0,2},{2,4},{4,6},{6,8},{8,10},{10,12},{12,14},{14,16},{16,18},{18... | collective-permute-start | bytes 1277960 | tf_op jit(solution)/shard_map/ppermute | solution.py:23
